TPU v7x, 32 devices: a whole 2x2x4 slice. The times are simulated.
32 devices in a mesh: groups: 2 (over y), rows: 16 (over z, x, core).
Axes of the slice: x: 2, y: 2, z: 4, core: 2. Of those that a mesh axis runs over, the one named last changes fastest.
Arguments:
- charges: bfloat16 [32768, 64], P(('groups', 'rows')), parts along dimension 0, may hold values from -6 to 6
- targets: bfloat16 [32768, 64], P(('groups', 'rows')), parts along dimension 0, may hold values from -6 to 6
- panel_order: int32 [32, 1024], P(('groups', 'rows')), parts along dimension 0, may hold values from 0 to 1023, each once within a row
- near_blocks: bfloat16 [2048, 128, 128], P(('groups', 'rows')), parts along dimension 0, may hold values from -0.1875 to 0.1875
- near_rows: int32 [2048], P(('groups', 'rows')), parts along dimension 0, may hold values from 0 to 7
- near_cols: int32 [2048], P(('groups', 'rows')), parts along dimension 0, may hold values from 0 to 9
- far_left: bfloat16 [512, 128, 32], P(('groups', 'rows')), parts along dimension 0, may hold values from -0.75 to 0.75
- far_right: bfloat16 [512, 128, 32], P(('groups', 'rows')), parts along dimension 0, may hold values from -0.5 to 0.5
- far_rows: int32 [512], P(('groups', 'rows')), parts along dimension 0, may hold values from 0 to 7
- far_slot: int32 [512], P(('groups', 'rows')), parts along dimension 0, may hold values from 0 to 63, as said below
- far_table: int32 [32, 64], P(('groups', 'rows')), parts along dimension 0, may hold values from -1 to 7, as said below
Outputs:
- potentials: bfloat16 [32768, 64], P(('groups', 'rows')), parts along dimension 0
- gradient: float32 [32768, 64], P(('groups', 'rows')), parts along dimension 0
There are 2 independent parts, one for each index of `groups`. A program takes and returns all parts, laid end to end along the dimension named above; each array names one. Nothing has to cross between parts.
Inputs may be any that keep to these rules, and one draw needn't show every extreme that they name: Per device, far_slot values are distinct; of the 16 far blocks of one device, 2 column owners hold 4 each, 2 hold two, 4 hold one and the rest none. far_table[s, t * 4 + k] is the local column cluster of device t's far block with slot s * 4 + k, and -1 exactly where device t has no such block.
All inputs are finite; a program needn't handle non-finite values.
Results may differ from a plain program's by a relative error of at most 0.0044.
Values may be sent and summed in bfloat16 or wider, within the bound.
A program may use at most 128 MiB of HBM per device.

v0:
```python
import jax
import jax.numpy as jnp
from jax import lax
from jax.sharding import PartitionSpec as P


def extended_2(value, sides, width):
    for axis, dim in sides:
        size, length = (lax.axis_size(axis), value.shape[dim])
        up = [(i, (i + 1) % size) for i in range(size - 1)]
        down = [(j, i) for i, j in up]
        last = lax.slice_in_dim(value, length - width, length, axis=dim)
        leading = lax.slice_in_dim(value, 0, width, axis=dim)
        before = lax.ppermute(last, axis, up)
        after = lax.ppermute(leading, axis, down)
        value = jnp.concatenate([before, value, after], axis=dim)
    return value


def shards(
    charges,
    targets,
    panel_order,
    near_blocks,
    near_rows,
    near_cols,
    far_left,
    far_right,
    far_rows,
    far_slot,
    far_table,
):
    row_devices = lax.axis_size("rows")
    block_size = near_blocks.shape[1]
    excite = charges.shape[1]
    cluster_count = charges.shape[0] // block_size
    slot_count = far_table.shape[1]
    permute = panel_order[0]
    ordered = jnp.take(charges, permute, axis=0)
    wanted = (
        jnp.take(targets, permute, axis=0)
        .astype(jnp.float32)
        .reshape(cluster_count, block_size, excite)
    )
    padded = extended_2(ordered, (("rows", 0),), block_size)
    extended = padded.reshape(cluster_count + 2, block_size, excite)
    near_out = jnp.einsum(
        "bij,bje->bie", near_blocks, extended[near_cols], preferred_element_type=jnp.float32
    )
    field = jnp.zeros((cluster_count, block_size, excite), jnp.float32).at[near_rows].add(near_out)
    table = far_table[0]
    live_slot = table >= 0
    safe_table = jnp.clip(table, 0, cluster_count - 1)
    local_blocks = ordered.reshape(cluster_count, block_size, excite)
    picked = local_blocks[safe_table]
    picked = jnp.where(live_slot[:, None, None], picked, jnp.array(0, jnp.bfloat16))
    arrived_cols = lax.all_to_all(
        picked.reshape(row_devices, -1, excite), "rows", split_axis=0, concat_axis=0, tiled=True
    )
    far_in = arrived_cols.reshape(slot_count, block_size, excite)[far_slot]
    coeffs = jnp.einsum(
        "bir,bie->bre", far_right, far_in, preferred_element_type=jnp.float32
    ).astype(jnp.bfloat16)
    far_out = jnp.einsum("bir,bre->bie", far_left, coeffs, preferred_element_type=jnp.float32)
    field = field.at[far_rows].add(far_out)
    misfit = (field - wanted).astype(jnp.bfloat16)
    near_back = jnp.einsum(
        "bij,bie->bje", near_blocks, misfit[near_rows], preferred_element_type=jnp.float32
    )
    ext_back = (
        jnp.zeros((cluster_count + 2, block_size, excite), jnp.float32).at[near_cols].add(near_back)
    )
    rim_terms = jnp.concatenate([ext_back[0], ext_back[-1]], axis=0)
    framed = extended_2(rim_terms.astype(jnp.bfloat16), (("rows", 0),), block_size).astype(
        rim_terms.dtype
    )
    back = ext_back[1:-1]
    back = back.at[0].add(framed[:block_size]).at[-1].add(framed[-block_size:])
    adjoint_coef = jnp.einsum(
        "bir,bie->bre", far_left, misfit[far_rows], preferred_element_type=jnp.float32
    ).astype(jnp.bfloat16)
    far_terms = jnp.einsum(
        "bir,bre->bie", far_right, adjoint_coef, preferred_element_type=jnp.float32
    )
    slot_terms = (
        jnp.zeros((slot_count, block_size, excite), jnp.float32).at[far_slot].set(far_terms)
    )
    arrived = lax.all_to_all(
        slot_terms.reshape(row_devices, -1, excite).astype(jnp.bfloat16),
        "rows",
        split_axis=0,
        concat_axis=0,
        tiled=True,
    ).astype(jnp.float32)
    arrived = arrived.reshape(slot_count, block_size, excite)
    arrived = jnp.where(live_slot[:, None, None], arrived, jnp.float32(0.0))
    back = back.at[safe_table].add(arrived)
    panel_total = cluster_count * block_size
    potentials = (
        jnp.zeros((panel_total, excite), jnp.bfloat16)
        .at[permute]
        .set(field.reshape(-1, excite).astype(jnp.bfloat16))
    )
    gradient = (
        jnp.zeros((panel_total, excite), jnp.float32).at[permute].set(back.reshape(-1, excite))
    )
    return (potentials, gradient)


def solution(mesh):
    in_specs = (
        P(("groups", "rows"), None),
        P(("groups", "rows"), None),
        P(("groups", "rows"), None),
        P(("groups", "rows"), None, None),
        P(("groups", "rows")),
        P(("groups", "rows")),
        P(("groups", "rows"), None, None),
        P(("groups", "rows"), None, None),
        P(("groups", "rows")),
        P(("groups", "rows")),
        P(("groups", "rows"), None),
    )
    out_specs = (P(("groups", "rows"), None), P(("groups", "rows"), None))
    return jax.shard_map(shards, mesh=mesh, in_specs=in_specs, out_specs=out_specs, check_vma=False)
```

profile of v0, /device:TPU:1, one launch (start us, length us, event | category | flops | bytes accessed | tf_op | source)
XLA Modules:
  0.0 129.0 jit_solution(16659121890163106513)
XLA Ops:
  0.6 0.8 fusion.8
  1.5 0.7 compare_and_fusion
  2.2 0.7 fusion.9
  2.8 1.2 compare_bitcast_fusion
  4.0 1.1 copy.81
  5.1 3.2 %gather_fusion.5 = bf16[1024,64]{1,0:T(8,128)(2,1)S(1)} fusion(bf16[1024,64]{1,0:T(8,128)(2,1)S(1)} %copy.81, s32[1024]{0:T(1024)S(1)} %fusion.8), kind=kCustom, calls=%fused_computation.clone | custom fusion | bytes 266240 | tf_op jit(solution)/shard_map/jit(_take)/gather | solution.py:39
  8.7 0.7 gather_fusion.1
  9.5 1.7 %copy.84 = bf16[64,128,64]{1,0,2:T(8,128)(2,1)} copy(bf16[64,128,64]{1,2,0:T(8,128)(2,1)S(1)} %gather_fusion.1) | data formatting | bytes 2097152 | tf_op jit(solution)/shard_map/gather | solution.py:55
  11.1 1.7 %gather.22 = bf16[16,512,64]{1,0,2:T(8,128)(2,1)S(1)} reshape(bf16[64,128,64]{1,0,2:T(8,128)(2,1)} %copy.84) | data formatting | bytes 2097152 | tf_op jit(solution)/shard_map/gather | solution.py:55
  13.2 1.6 %copy.85 = bf16[16,512,64]{1,2,0:T(8,128)(2,1)} copy(bf16[16,512,64]{1,0,2:T(8,128)(2,1)S(1)} %broadcast_select_fusion) | data formatting | bytes 2097152 | tf_op jit(solution)/shard_map/jit(_where)/select_n | solution.py:56
  14.7 7.3 %all-to-all-start = ((bf16[16,512,64]{1,2,0:T(8,128)(2,1)}), bf16[16,512,64]{1,2,0:T(8,128)(2,1)}, u32[]{:S(2)}, u32[]{:S(2)}) async-start(bf16[16,512,64]{1,2,0:T(8,128)(2,1)} %copy.85), calls=%async_computation | async-start | bytes 2097152 | tf_op jit(solution)/shard_map/all_to_all | solution.py:57
  22.1 3.5 %collective-permute-start = (bf16[128,64]{1,0:T(8,128)(2,1)S(1)}, bf16[128,64]{1,0:T(8,128)(2,1)S(1)}, u32[]{:S(2)}, u32[]{:S(2)}) collective-permute-start(bf16[128,64]{1,0:T(8,128)(2,1)S(1)} %get-tuple-element.39), channel_id=1, source_target_pairs={{0,1},{1,2},{2,3},{3,4},{4,5},{5,6},{6,7},{7,8},{8,9},{9,10},{10,1... | collective-permute-start | bytes 49160 | tf_op jit(solution)/shard_map/ppermute | solution.py:14
  25.6 1.9 %collective-permute-start.1 = (bf16[128,64]{1,0:T(8,128)(2,1)S(1)}, bf16[128,64]{1,0:T(8,128)(2,1)S(1)}, u32[]{:S(2)}, u32[]{:S(2)}) collective-permute-start(bf16[128,64]{1,0:T(8,128)(2,1)S(1)} %get-tuple-element.40), channel_id=1, source_target_pairs={{1,0},{2,1},{3,2},{4,3},{5,4},{6,5},{7,6},{8,7},{9,8},{10,9},{11,1... | collective-permute-start | bytes 49160 | tf_op jit(solution)/shard_map/ppermute | solution.py:15
  27.6 0.6 pad_clamp_fusion.4
  29.4 3.2 %gather_fusion.6 = bf16[1024,64]{1,0:T(8,128)(2,1)S(1)} fusion(bf16[1024,64]{1,0:T(8,128)(2,1)S(1)} %copy.90, s32[1024]{0:T(1024)S(1)} %fusion.8), kind=kCustom, calls=%fused_computation.1.clone | custom fusion | bytes 266240 | tf_op jit(solution)/shard_map/jit(_take)/gather | solution.py:41
  32.6 0.8 copy.91
  33.7 0.9 gather_fusion
  34.6 2.9 %convolution_bitcast_fusion.1 = f32[64,128,64]{1,2,0:T(8,128)} fusion(bf16[64,128,64]{1,2,0:T(8,128)(2,1)S(1)} %gather_fusion, bf16[64,128,128]{2,1,0:T(8,128)(2,1)S(1)} %copy-done), kind=kOutput, calls=%fused_computation.16 | convolution fusion | flops 134217728 | bytes 5242880 | tf_op jit(solution)/shard_map/bij,bje->bie/dot_general | solution.py:47
  37.5 7.0 %scatter_fusion = f32[8,128,64]{1,2,0:T(8,128)S(1)} fusion(f32[8,128,64]{1,2,0:T(8,128)S(1)} %broadcast_in_dim.73, s32[64]{0:T(128)S(1)} %copy-done.11, f32[64,128,64]{1,2,0:T(8,128)} %convolution_bitcast_fusion.1), kind=kCustom, calls=%fused_computation.7 | custom fusion | flops 524288 | bytes 6291712 | tf_op jit(solution)/shard_map/scatter-add | solution.py:50
  44.5 0.8 all-to-all-done
  45.3 1.8 %copy.86 = bf16[16,512,64]{1,0,2:T(8,128)(2,1)S(1)} copy(bf16[16,512,64]{1,2,0:T(8,128)(2,1)} %all-to-all-done) | data formatting | bytes 2097152 | tf_op jit(solution)/shard_map/all_to_all | solution.py:57
  47.1 1.5 %reshape.167 = bf16[64,128,64]{1,0,2:T(8,128)(2,1)} reshape(bf16[16,512,64]{1,0,2:T(8,128)(2,1)S(1)} %copy.86) | data formatting | bytes 2097152 | tf_op jit(solution)/shard_map/reshape | solution.py:60
  48.6 1.9 %copy.87 = bf16[64,128,64]{1,2,0:T(8,128)(2,1)S(1)} copy(bf16[64,128,64]{1,0,2:T(8,128)(2,1)} %reshape.167) | data formatting | bytes 2097152 | tf_op jit(solution)/shard_map/reshape | solution.py:60
  50.5 1.3 gather_fusion.2
  51.8 1.5 %convolution_bitcast_fusion.3 = f32[16,128,64]{1,2,0:T(8,128)S(1)} fusion(bf16[16,128,32]{1,2,0:T(8,128)(2,1)S(1)} %copy-done.2, bf16[16,128,64]{1,2,0:T(8,128)(2,1)} %gather_fusion.2, bf16[16,128,32]{1,2,0:T(8,128)(2,1)} %param.24), kind=kOutput, calls=%fused_computation.18 | convolution fusion | flops 16809984 | bytes 1048576 | tf_op jit(solution)/shard_map/bir,bre->bie/dot_general | solution.py:64
  53.3 1.5 %scatter_fusion.1 = f32[8,128,64]{1,2,0:T(8,128)S(1)} fusion(f32[8,128,64]{1,2,0:T(8,128)S(1)} %scatter_fusion, s32[16]{0:T(128)} %copy-done.14, f32[16,128,64]{1,2,0:T(8,128)S(1)} %convolution_bitcast_fusion.3), kind=kCustom, calls=%fused_computation.8 | custom fusion | flops 131072 | bytes 1572928 | tf_op jit(solution)/shard_map/scatter-add | solution.py:65
  54.9 0.6 gather_fusion.4
  55.9 1.6 %broadcast_in_dim.85 = f32[64,128,64]{1,2,0:T(8,128)} broadcast(f32[]{:T(128)} %constant.83.clone.1), dimensions={} | broadcast | bytes 2097156 | tf_op jit(solution)/shard_map/broadcast_in_dim | solution.py:86
  57.5 2.6 %scatter_fusion.3 = f32[64,128,64]{1,2,0:T(8,128)} fusion(f32[64,128,64]{1,2,0:T(8,128)} %broadcast_in_dim.85, s32[16]{0:T(128)S(1)} %copy-done.13, f32[16,128,64]{1,2,0:T(8,128)S(1)} %convolution_bitcast_fusion.2), kind=kCustom, calls=%fused_computation.11 | custom fusion | bytes 1572928 | tf_op jit(solution)/shard_map/scatter | solution.py:86
  60.1 1.8 %convert_element_type.35 = bf16[64,128,64]{1,2,0:T(8,128)(2,1)S(1)} convert(f32[64,128,64]{1,2,0:T(8,128)} %scatter_fusion.3) | non-fusion elementwise | flops 524288 | bytes 3145728 | tf_op jit(solution)/shard_map/convert_element_type | solution.py:89
  61.9 0.7 copy.93
  62.6 1.5 %convert_element_type.36 = bf16[16,512,64]{1,0,2:T(8,128)(2,1)} reshape(bf16[64,128,64]{1,0,2:T(8,128)(2,1)S(1)} %copy.93) | data formatting | bytes 2097152 | tf_op jit(solution)/shard_map/convert_element_type | solution.py:89
  64.1 2.8 %copy.94 = bf16[16,512,64]{1,2,0:T(8,128)(2,1)} copy(bf16[16,512,64]{1,0,2:T(8,128)(2,1)} %convert_element_type.36) | data formatting | bytes 2097152 | tf_op jit(solution)/shard_map/convert_element_type | solution.py:89
  66.9 17.4 %all-to-all-start.1 = ((bf16[16,512,64]{1,2,0:T(8,128)(2,1)}), bf16[16,512,64]{1,2,0:T(8,128)(2,1)}, u32[]{:S(2)}, u32[]{:S(2)}) async-start(bf16[16,512,64]{1,2,0:T(8,128)(2,1)} %copy.94), calls=%async_computation.1 | async-start | bytes 2097152 | tf_op jit(solution)/shard_map/all_to_all | solution.py:88
  84.3 0.7 gather_fusion.3
  85.1 2.0 %convolution_bitcast_fusion = f32[64,128,64]{1,2,0:T(8,128)} fusion(bf16[64,128,64]{1,2,0:T(8,128)(2,1)S(1)} %gather_fusion.3, bf16[64,128,128]{2,1,0:T(8,128)(2,1)S(1)} %copy-done), kind=kOutput, calls=%fused_computation.15 | convolution fusion | flops 134217728 | bytes 5242880 | tf_op jit(solution)/shard_map/bij,bie->bje/dot_general | solution.py:67
  87.1 7.0 %scatter_fusion.2 = f32[10,128,64]{1,2,0:T(8,128)S(1)} fusion(f32[10,128,64]{1,2,0:T(8,128)S(1)} %broadcast_in_dim.83, s32[64]{0:T(128)S(1)} %copy-done.10, f32[64,128,64]{1,2,0:T(8,128)} %convolution_bitcast_fusion), kind=kCustom, calls=%fused_computation.10 | custom fusion | flops 524288 | bytes 6291712 | tf_op jit(solution)/shard_map/scatter-add | solution.py:71
  94.2 3.5 %collective-permute-start.2 = (bf16[128,64]{0,1:T(8,128)(2,1)S(1)}, bf16[128,64]{0,1:T(8,128)(2,1)S(1)}, u32[]{:S(2)}, u32[]{:S(2)}) collective-permute-start(bf16[128,64]{0,1:T(8,128)(2,1)S(1)} %get-tuple-element.41), channel_id=1, source_target_pairs={{0,1},{1,2},{2,3},{3,4},{4,5},{5,6},{6,7},{7,8},{8,9},{9,10},{10,1... | collective-permute-start | bytes 49160 | tf_op jit(solution)/shard_map/ppermute | solution.py:14
  97.8 1.9 %collective-permute-start.3 = (bf16[128,64]{0,1:T(8,128)(2,1)S(1)}, bf16[128,64]{0,1:T(8,128)(2,1)S(1)}, u32[]{:S(2)}, u32[]{:S(2)}) collective-permute-start(bf16[128,64]{0,1:T(8,128)(2,1)S(1)} %get-tuple-element.42), channel_id=1, source_target_pairs={{1,0},{2,1},{3,2},{4,3},{5,4},{6,5},{7,6},{8,7},{9,8},{10,9},{11,1... | collective-permute-start | bytes 49160 | tf_op jit(solution)/shard_map/ppermute | solution.py:15
  100.0 3.2 %scatter_custom_fusion.2 = bf16[1024,64]{1,0:T(8,128)(2,1)S(1)} fusion(s32[1024]{0:T(1024)S(1)} %bitcast.71, bf16[1024,64]{1,0:T(8,128)(2,1)S(1)} %bitcast.66, bf16[]{:T(256)} %constant.80.clone.1), kind=kCustom, calls=%fused_computation.29 | custom fusion | bytes 131074 | tf_op jit(solution)/shard_map/scatter | solution.py:102
  103.2 0.8 copy.99
  104.0 3.5 %all-to-all-done.1 = bf16[16,512,64]{1,2,0:T(8,128)(2,1)} async-done(((bf16[16,512,64]{1,2,0:T(8,128)(2,1)}), bf16[16,512,64]{1,2,0:T(8,128)(2,1)}, u32[]{:S(2)}, u32[]{:S(2)}) %all-to-all-start.1) | async-done | bytes 1048608 | tf_op jit(solution)/shard_map/all_to_all | solution.py:88
  107.6 3.1 %copy.95 = f32[16,512,64]{1,0,2:T(8,128)} copy(bf16[16,512,64]{1,2,0:T(8,128)(2,1)} %all-to-all-done.1) | data formatting | bytes 3145728 | tf_op jit(solution)/shard_map/reshape | solution.py:95
  110.7 2.6 %reshape.178 = f32[64,128,64]{1,0,2:T(8,128)} reshape(f32[16,512,64]{1,0,2:T(8,128)} %copy.95) | data formatting | bytes 4194304 | tf_op jit(solution)/shard_map/reshape | solution.py:95
  113.3 4.3 %copy_select_fusion = f32[64,128,64]{1,2,0:T(8,128)} fusion(f32[64,128,64]{1,0,2:T(8,128)} %reshape.178, pred[64]{0:T(512)(128)(4,1)S(1)} %copy-done.15), kind=kLoop, calls=%fused_computation.14 | loop fusion | flops 524288 | bytes 4194368 | tf_op jit(solution)/shard_map/jit(_where)/select_n | solution.py:96
  117.6 7.1 %scatter_fusion.4 = f32[8,128,64]{1,2,0:T(8,128)S(1)} fusion(f32[8,128,64]{1,2,0:T(8,128)S(1)} %fusion.5, s32[64]{0:T(128)S(1)} %copy-done.8, f32[64,128,64]{1,2,0:T(8,128)} %copy_select_fusion), kind=kCustom, calls=%fused_computation.12 | custom fusion | flops 524288 | bytes 6291712 | tf_op jit(solution)/shard_map/scatter-add | solution.py:97
  124.9 3.2 %scatter_custom_fusion.6 = f32[1024,64]{1,0:T(8,128)S(1)} fusion(s32[1024]{0:T(1024)S(1)} %bitcast.72, f32[1024,64]{1,0:T(8,128)S(1)} %bitcast.65, f32[]{:T(128)} %constant.83.clone.1), kind=kCustom, calls=%fused_computation.26 | custom fusion | bytes 262148 | tf_op jit(solution)/shard_map/scatter | solution.py:105
  128.1 0.9 copy.100
  (74 shorter events, 3.1 us)
Async XLA Ops:
  0.6 33.9 %copy-start = (bf16[64,128,128]{2,1,0:T(8,128)(2,1)S(1)}, bf16[64,128,128]{2,1,0:T(8,128)(2,1)}, u32[]{:S(2)}) copy-start(bf16[64,128,128]{2,1,0:T(8,128)(2,1)} %param.20) | copy-start | bytes 6291460
  2.8 5.8 %copy-start.7 = (s32[64]{0:T(128)}, s32[64]{0:T(128)S(1)}, u32[]{:S(2)}) copy-start(s32[64]{0:T(128)S(1)} %fusion.9) | copy-start | bytes 772
  13.1 14.4 %copy-start.16 = (s32[64]{0:T(128)S(1)}, s32[64]{0:T(128)}, u32[]{:S(2)}) copy-start(s32[64]{0:T(128)} %param.22) | copy-start | bytes 772
  13.1 15.1 %copy-start.17 = (s32[16]{0:T(128)S(1)}, s32[16]{0:T(128)}, u32[]{:S(2)}) copy-start(s32[16]{0:T(128)} %param.26) | copy-start | bytes 196
  13.1 15.1 %copy-start.18 = (s32[64]{0:T(128)S(1)}, s32[64]{0:T(128)}, u32[]{:S(2)}) copy-start(s32[64]{0:T(128)} %param.21) | copy-start | bytes 772
  13.1 15.6 %copy-start.19 = (s32[16]{0:T(128)S(1)}, s32[16]{0:T(128)}, u32[]{:S(2)}) copy-start(s32[16]{0:T(128)} %param.25) | copy-start | bytes 196
  13.2 16.1 %copy-start.5 = (bf16[1024,64]{0,1:T(8,128)(2,1)S(1)}, bf16[1024,64]{0,1:T(8,128)(2,1)}, u32[]{:S(2)}) copy-start(bf16[1024,64]{0,1:T(8,128)(2,1)} %param.18) | copy-start | bytes 393220
  14.7 30.6 %all-to-all-start = ((bf16[16,512,64]{1,2,0:T(8,128)(2,1)}), bf16[16,512,64]{1,2,0:T(8,128)(2,1)}, u32[]{:S(2)}, u32[]{:S(2)}) async-start(bf16[16,512,64]{1,2,0:T(8,128)(2,1)} %copy.85), calls=%async_computation | async-start | bytes 2097152 | tf_op jit(solution)/shard_map/all_to_all | solution.py:57
  22.1 11.4 %collective-permute-start = (bf16[128,64]{1,0:T(8,128)(2,1)S(1)}, bf16[128,64]{1,0:T(8,128)(2,1)S(1)}, u32[]{:S(2)}, u32[]{:S(2)}) collective-permute-start(bf16[128,64]{1,0:T(8,128)(2,1)S(1)} %get-tuple-element.39), channel_id=1, source_target_pairs={{0,1},{1,2},{2,3},{3,4},{4,5},{5,6},{6,7},{7,8},{8,9},{9,10},{10,1... | collective-permute-start | bytes 49160 | tf_op jit(solution)/shard_map/ppermute | solution.py:14
  25.6 7.8 %collective-permute-start.1 = (bf16[128,64]{1,0:T(8,128)(2,1)S(1)}, bf16[128,64]{1,0:T(8,128)(2,1)S(1)}, u32[]{:S(2)}, u32[]{:S(2)}) collective-permute-start(bf16[128,64]{1,0:T(8,128)(2,1)S(1)} %get-tuple-element.40), channel_id=1, source_target_pairs={{1,0},{2,1},{3,2},{4,3},{5,4},{6,5},{7,6},{8,7},{9,8},{10,9},{11,1... | collective-permute-start | bytes 49160 | tf_op jit(solution)/shard_map/ppermute | solution.py:15
  27.6 1.2 copy-start.9
  28.2 0.5 copy-start.12
  28.7 0.5 copy-start.14
  34.6 2.9 %copy-start.11 = (s32[64]{0:T(128)S(1)}, s32[64]{0:T(128)}, u32[]{:S(2)}) copy-start(s32[64]{0:T(128)} %compare_select_fusion.6) | copy-start | bytes 772
  48.6 3.2 %copy-start.2 = (bf16[16,128,32]{1,2,0:T(8,128)(2,1)S(1)}, bf16[16,128,32]{1,2,0:T(8,128)(2,1)}, u32[]{:S(2)}) copy-start(bf16[16,128,32]{1,2,0:T(8,128)(2,1)} %param.23) | copy-start | bytes 393220
  51.8 3.0 %copy-start.1 = (bf16[1024,64]{0,1:T(8,128)(2,1)S(1)}, bf16[1024,64]{0,1:T(8,128)(2,1)}, u32[]{:S(2)}) copy-start(bf16[1024,64]{0,1:T(8,128)(2,1)} %copy.91) | copy-start | bytes 393220
  51.8 3.7 %copy-start.3 = (bf16[16,128,32]{1,2,0:T(8,128)(2,1)S(1)}, bf16[16,128,32]{1,2,0:T(8,128)(2,1)}, u32[]{:S(2)}) copy-start(bf16[16,128,32]{1,2,0:T(8,128)(2,1)} %param.23) | copy-start | bytes 393220
  51.8 3.7 %copy-start.4 = (bf16[16,128,32]{1,2,0:T(8,128)(2,1)S(1)}, bf16[16,128,32]{1,2,0:T(8,128)(2,1)}, u32[]{:S(2)}) copy-start(bf16[16,128,32]{1,2,0:T(8,128)(2,1)} %param.24) | copy-start | bytes 393220
  54.8 2.7 %copy-start.13 = (s32[16]{0:T(128)S(1)}, s32[16]{0:T(128)}, u32[]{:S(2)}) copy-start(s32[16]{0:T(128)} %copy-done.12) | copy-start | bytes 196
  66.9 40.7 %all-to-all-start.1 = ((bf16[16,512,64]{1,2,0:T(8,128)(2,1)}), bf16[16,512,64]{1,2,0:T(8,128)(2,1)}, u32[]{:S(2)}, u32[]{:S(2)}) async-start(bf16[16,512,64]{1,2,0:T(8,128)(2,1)} %copy.94), calls=%async_computation.1 | async-start | bytes 2097152 | tf_op jit(solution)/shard_map/all_to_all | solution.py:88
  85.1 2.0 %copy-start.10 = (s32[64]{0:T(128)S(1)}, s32[64]{0:T(128)}, u32[]{:S(2)}) copy-start(s32[64]{0:T(128)} %copy-done.9) | copy-start | bytes 772
  87.1 12.6 %copy-start.6 = (s32[1,1024]{1,0:T(1,128)S(1)}, s32[1,1024]{1,0:T(1,128)}, u32[]{:S(2)}) copy-start(s32[1,1024]{1,0:T(1,128)} %param.19) | copy-start | bytes 12292
  94.2 9.7 %collective-permute-start.2 = (bf16[128,64]{0,1:T(8,128)(2,1)S(1)}, bf16[128,64]{0,1:T(8,128)(2,1)S(1)}, u32[]{:S(2)}, u32[]{:S(2)}) collective-permute-start(bf16[128,64]{0,1:T(8,128)(2,1)S(1)} %get-tuple-element.41), channel_id=1, source_target_pairs={{0,1},{1,2},{2,3},{3,4},{4,5},{5,6},{6,7},{7,8},{8,9},{9,10},{10,1... | collective-permute-start | bytes 49160 | tf_op jit(solution)/shard_map/ppermute | solution.py:14
  97.8 6.2 %collective-permute-start.3 = (bf16[128,64]{0,1:T(8,128)(2,1)S(1)}, bf16[128,64]{0,1:T(8,128)(2,1)S(1)}, u32[]{:S(2)}, u32[]{:S(2)}) collective-permute-start(bf16[128,64]{0,1:T(8,128)(2,1)S(1)} %get-tuple-element.42), channel_id=1, source_target_pairs={{1,0},{2,1},{3,2},{4,3},{5,4},{6,5},{7,6},{8,7},{9,8},{10,9},{11,1... | collective-permute-start | bytes 49160 | tf_op jit(solution)/shard_map/ppermute | solution.py:15
  110.7 2.6 %copy-start.15 = (pred[64]{0:T(512)(128)(4,1)S(1)}, pred[64]{0:T(512)(128)(4,1)}, u32[]{:S(2)}) copy-start(pred[64]{0:T(512)(128)(4,1)} %get-tuple-element.43) | copy-start | bytes 196
  113.3 4.3 %copy-start.8 = (s32[64]{0:T(128)S(1)}, s32[64]{0:T(128)}, u32[]{:S(2)}) copy-start(s32[64]{0:T(128)} %copy-done.7) | copy-start | bytes 772
where the time goes:
time: 131 us; the launch traced here: 129 us
  local copies, waits for them, and re-layouts  47.4 us (36%)
  starting transfers between devices  35.7 us (27%)
  other arithmetic  33.7 us (26%)
  matrix products  6.8 us (5%)
  waiting for transfers between devices  4.33 us (3%)
    all_to_all x1, starting transfers between devices, shards(): lax.all_to_all(slot_terms.reshape(row_devices, -1, excite).astype(jnp.bfl...  17.4 us
    all_to_all x1, starting transfers between devices, shards(): lax.all_to_all(picked.reshape(row_devices, -1, excite), 'rows', split_axi...  7.32 us
    ppermute x2, starting transfers between devices, extended_2(): before = lax.ppermute(last, axis, up)  7.09 us
    scatter-add x1, other arithmetic, shards(): back = back.at[safe_table].add(arrived)  7.06 us
    scatter-add x1, other arithmetic, shards(): jnp.zeros((cluster_count, block_size, excite), jnp.float32).at[near_rows]  7.05 us
    scatter-add x1, other arithmetic, shards(): jnp.zeros((cluster_count + 2, block_size, excite), jnp.float32)  7.04 us
    reshape x2, local copies, waits for them, and re-layouts, shards(): arrived = arrived.reshape(slot_count, block_size, excite)  5.76 us
    convert_element_type x3, local copies, waits for them, and re-layouts, shards(): slot_terms.reshape(row_devices, -1, excite).astype(jnp.bfloat16)  4.94 us
  transfers between devices with their start and end apart: 6, of which 2 were waited for; matrix products, arithmetic and copies ran while one was open for 24% of the time, Pallas kernels for 0%

commit v1 on v0

v1 whole, which is shorter than its diff:
```python
import functools

import jax
import jax.numpy as jnp
from jax import lax
from jax.experimental import pallas as pl
from jax.experimental.pallas import tpu as pltpu
from jax.sharding import PartitionSpec as P

BF = jnp.bfloat16
F32 = jnp.float32
GROUP = 4


def dot(a, b, ca, cb):
    return lax.dot_general(a, b, (((ca,), (cb,)), ((), ())), preferred_element_type=F32)


def kernel(
    n,
    charges,
    targets,
    order,
    near_hbm,
    nrows,
    ncols,
    fleft,
    fright,
    frows,
    fslot,
    ftable,
    pot,
    grad,
    near,
    pt,
    ext,
    want,
    fr4,
    fl4,
    rslot,
    rin,
    lslot,
    cbuf,
    cin,
    abuf,
    ain,
    field,
    misfit,
    back,
    rimbuf,
    rimin,
    rowtab,
    near_sem,
    r_send,
    r_recv,
    c_send,
    c_recv,
    a_send,
    a_recv,
    e_send,
    e_recv,
    b_send,
    b_recv,
):
    me = lax.axis_index("rows")
    left, right = me - 1, me + 1
    panels, exc = charges.shape
    nears, leaf, _ = near.shape
    fars, _, rank = fleft.shape
    cap = ftable.shape[1] // n
    cl = panels // leaf
    wide = cap * rank

    near_copy = pltpu.make_async_copy(near_hbm, near, near_sem)
    near_copy.start()
    barrier = pltpu.get_barrier_semaphore()

    @pl.loop(1, n)
    def _(d):
        pl.semaphore_signal(
            barrier,
            inc=1,
            device_id={"rows": lax.rem(me + d, n)},
            device_id_type=pl.DeviceIdType.MESH,
        )

    lane_slot = lax.broadcasted_iota(jnp.int32, (1, wide), 1) // rank
    spread = (
        lax.broadcasted_iota(jnp.int32, (rank, wide), 0)
        == lax.broadcasted_iota(jnp.int32, (rank, wide), 1) % rank
    ).astype(F32).astype(BF)
    fr4[...] = dot(fright[...].reshape(fars * leaf, rank), spread, 1, 0).astype(BF).reshape(fars, leaf, wide)

    def place(table, s):
        slots = lane_slot + s * cap

        def some(g, acc):
            for k in range(16):
                b = g * 16 + k
                hot = (slots == fslot[b]).astype(F32).astype(BF)
                acc = acc + table[b] * hot
            return acc

        zero = jnp.zeros((leaf, wide), BF)
        if fars == 16:
            return some(0, zero)
        return lax.fori_loop(0, fars // 16, some, zero)

    def send(src, dst, send_sem, recv_sem, d):
        return pltpu.make_async_remote_copy(
            src_ref=src,
            dst_ref=dst,
            send_sem=send_sem,
            recv_sem=recv_sem,
            device_id={"rows": d},
            device_id_type=pl.DeviceIdType.MESH,
        )

    @pl.loop(0, n)
    def _(s):
        rslot[s] = place(fr4, s)

    rin[me] = rslot[me]
    pl.semaphore_wait(barrier, n - 1)

    @pl.loop(1, n)
    def _(d):
        t = lax.rem(me + d, n)
        send(rslot.at[t], rin.at[me], r_send.at[d], r_recv.at[d], t).start()

    pt[...] = (
        lax.broadcasted_iota(jnp.int32, (panels, panels), 0) == order[...]
    ).astype(F32).astype(BF)
    both = jnp.concatenate([charges[...], targets[...]], axis=1)
    sorted_t = dot(both, pt[...], 0, 0).astype(BF)
    for c in range(cl):
        ext[c + 1] = sorted_t[:exc, c * leaf : (c + 1) * leaf]
        want[pl.ds(c * exc, exc), :] = sorted_t[exc:, c * leaf : (c + 1) * leaf].astype(F32)

    to_left = send(ext.at[1], ext.at[cl + 1], e_send.at[0], e_recv.at[0], left)
    to_right = send(ext.at[cl], ext.at[0], e_send.at[1], e_recv.at[1], right)

    @pl.when(me > 0)
    def _():
        to_left.start()

    @pl.when(me < n - 1)
    def _():
        to_right.start()

    fl4[...] = dot(fleft[...].reshape(fars * leaf, rank), spread, 1, 0).astype(BF).reshape(fars, leaf, wide)

    @pl.loop(0, n)
    def _(s):
        lslot[s] = place(fl4, s)
        slots = lane_slot + s * cap

        def some(g, acc):
            for k in range(16):
                b = g * 16 + k
                acc = jnp.where(slots == fslot[b], frows[b], acc)
            return acc

        rowtab[pl.ds(s, 1), :] = lax.fori_loop(0, fars // 16, some, jnp.zeros((1, wide), jnp.int32))

    @pl.when(me < n - 1)
    def _():
        to_left.wait_recv()

    @pl.when(me == n - 1)
    def _():
        ext[cl + 1] = jnp.zeros((exc, leaf), BF)

    @pl.when(me > 0)
    def _():
        to_right.wait_recv()

    @pl.when(me == 0)
    def _():
        ext[0] = jnp.zeros((exc, leaf), BF)

    near_copy.wait()
    nothing = jnp.zeros((exc, leaf), BF)

    def stacked(value, place_of, count):
        return jnp.concatenate(
            [lax.select(place_of == r, value, nothing) for r in range(count)], axis=0
        )

    field[...] = jnp.zeros(field.shape, F32)

    @pl.loop(0, nears // GROUP)
    def _(g):
        ins, blocks = [], []
        for k in range(GROUP):
            b = g * GROUP + k
            ins.append(stacked(ext[ncols[b]], nrows[b], cl))
            blocks.append(near[b])
        field[...] += dot(jnp.concatenate(ins, axis=1), jnp.concatenate(blocks, axis=1), 1, 1)

    def owner_row(t):
        row = jnp.full((1, wide), -1, jnp.int32)
        for k in range(cap):
            row = jnp.where(lane_slot == k, ftable[0, t * cap + k], row)
        return row

    def chosen(product, row):
        total = jnp.zeros((exc, wide), F32)
        for c in range(cl):
            total = total + jnp.where(row == c, product[c * exc : (c + 1) * exc], 0.0)
        return total.astype(BF)

    def expanded(value, row):
        return jnp.concatenate(
            [value * (row == c).astype(F32).astype(BF) for c in range(cl)], axis=0
        )

    def coefs(t):
        return chosen(dot(ext[1 : cl + 1].reshape(cl * exc, leaf), rin[t], 1, 0), owner_row(t))

    cin[me] = coefs(me)

    @pl.loop(1, n)
    def _(d):
        t = lax.rem(me + n - d, n)
        send(rslot.at[me], rin.at[t], r_send.at[d], r_recv.at[d], t).wait_recv()
        cbuf[t] = coefs(t)
        send(cbuf.at[t], cin.at[me], c_send.at[d], c_recv.at[d], t).start()

    def far_out(s):
        field[...] += dot(expanded(cin[s], rowtab[pl.ds(s, 1), :]), lslot[s], 1, 1)

    far_out(me)

    @pl.loop(1, n)
    def _(d):
        s = lax.rem(me + d, n)
        send(cbuf.at[s], cin.at[s], c_send.at[d], c_recv.at[d], s).wait_recv()
        far_out(s)

    misfit[...] = (field[...] - want[...]).astype(BF).reshape(misfit.shape)

    def adjoint(s):
        product = dot(misfit[...].reshape(cl * exc, leaf), lslot[s], 1, 0)
        return chosen(product, rowtab[pl.ds(s, 1), :])

    @pl.loop(1, n)
    def _(d):
        s = lax.rem(me + d, n)
        abuf[s] = adjoint(s)
        send(abuf.at[s], ain.at[me], a_send.at[d], a_recv.at[d], s).start()

    ain[me] = adjoint(me)

    back[...] = jnp.zeros(back.shape, F32)

    @pl.loop(0, nears // GROUP)
    def _(g):
        ins = [
            stacked(misfit[nrows[g * GROUP + k]], ncols[g * GROUP + k], cl + 2)
            for k in range(GROUP)
        ]
        blocks = near[pl.ds(g * GROUP, GROUP)].reshape(GROUP * leaf, leaf)
        back[...] += dot(jnp.concatenate(ins, axis=1), blocks, 1, 0)

    rimbuf[0] = back[:exc].astype(BF)
    rimbuf[1] = back[(cl + 1) * exc :].astype(BF)
    rim_left = send(rimbuf.at[0], rimin.at[1], b_send.at[0], b_recv.at[0], left)
    rim_right = send(rimbuf.at[1], rimin.at[0], b_send.at[1], b_recv.at[1], right)

    @pl.when(me > 0)
    def _():
        rim_left.start()

    @pl.when(me < n - 1)
    def _():
        rim_right.start()

    inner = pl.ds(exc, cl * exc)

    def far_back(t):
        back[inner, :] += dot(expanded(ain[t], owner_row(t)), rin[t], 1, 1)

    far_back(me)

    @pl.loop(1, n)
    def _(d):
        t = lax.rem(me + n - d, n)
        send(abuf.at[t], ain.at[t], a_send.at[d], a_recv.at[d], t).wait_recv()
        far_back(t)

    @pl.when(me < n - 1)
    def _():
        rim_left.wait_recv()
        back[pl.ds(cl * exc, exc), :] += rimin[1].astype(F32)

    @pl.when(me > 0)
    def _():
        rim_right.wait_recv()
        back[pl.ds(exc, exc), :] += rimin[0].astype(F32)

    def flat(value):
        return jnp.concatenate([value[c * exc : (c + 1) * exc] for c in range(cl)], axis=1)

    full = flat(back[inner, :])
    high = full.astype(BF)
    rest = full - high.astype(F32)
    mid = rest.astype(BF)
    low = (rest - mid.astype(F32)).astype(BF)
    parts = jnp.concatenate([high, mid, flat(field[...]).astype(BF), low], axis=0)
    result = dot(pt[...], parts, 1, 1)
    pot[...] = result[:, 2 * exc : 3 * exc].astype(BF)
    grad[...] = (result[:, exc : 2 * exc] + result[:, 3 * exc :]) + result[:, :exc]

    @pl.loop(1, n)
    def _(d):
        t = lax.rem(me + d, n)
        s = lax.rem(me + n - d, n)
        send(rslot.at[t], rin.at[me], r_send.at[d], r_recv.at[d], t).wait_send()
        send(cbuf.at[s], cin.at[me], c_send.at[d], c_recv.at[d], s).wait_send()
        send(abuf.at[t], ain.at[me], a_send.at[d], a_recv.at[d], t).wait_send()

    @pl.when(me > 0)
    def _():
        to_left.wait_send()
        rim_left.wait_send()

    @pl.when(me < n - 1)
    def _():
        to_right.wait_send()
        rim_right.wait_send()


def shards(
    charges,
    targets,
    panel_order,
    near_blocks,
    near_rows,
    near_cols,
    far_left,
    far_right,
    far_rows,
    far_slot,
    far_table,
):
    n = lax.axis_size("rows")
    panels, exc = charges.shape
    nears, leaf, _ = near_blocks.shape
    fars, _, rank = far_left.shape
    cl = panels // leaf
    wide = far_table.shape[1] // n * rank
    vmem = pl.BlockSpec(memory_space=pltpu.VMEM)
    smem = pl.BlockSpec(memory_space=pltpu.SMEM)
    anywhere = pl.BlockSpec(memory_space=pl.ANY)
    sems = pltpu.SemaphoreType.DMA((n,))
    pair = pltpu.SemaphoreType.DMA((2,))
    return pl.pallas_call(
        functools.partial(kernel, n),
        out_shape=(
            jax.ShapeDtypeStruct((panels, exc), BF),
            jax.ShapeDtypeStruct((panels, exc), F32),
        ),
        in_specs=[vmem, vmem, vmem, anywhere, smem, smem, vmem, vmem, smem, smem, smem],
        out_specs=(vmem, vmem),
        scratch_shapes=[
            pltpu.VMEM((nears, leaf, leaf), BF),
            pltpu.VMEM((panels, panels), BF),
            pltpu.VMEM((cl + 2, exc, leaf), BF),
            pltpu.VMEM((cl * exc, leaf), F32),
            pltpu.VMEM((fars, leaf, wide), BF),
            pltpu.VMEM((fars, leaf, wide), BF),
            pltpu.VMEM((n, leaf, wide), BF),
            pltpu.VMEM((n, leaf, wide), BF),
            pltpu.VMEM((n, leaf, wide), BF),
            pltpu.VMEM((n, exc, wide), BF),
            pltpu.VMEM((n, exc, wide), BF),
            pltpu.VMEM((n, exc, wide), BF),
            pltpu.VMEM((n, exc, wide), BF),
            pltpu.VMEM((cl * exc, leaf), F32),
            pltpu.VMEM((cl, exc, leaf), BF),
            pltpu.VMEM(((cl + 2) * exc, leaf), F32),
            pltpu.VMEM((2, exc, leaf), BF),
            pltpu.VMEM((2, exc, leaf), BF),
            pltpu.VMEM((n, wide), jnp.int32),
            pltpu.SemaphoreType.DMA,
            sems,
            sems,
            sems,
            sems,
            sems,
            sems,
            pair,
            pair,
            pair,
            pair,
        ],
        compiler_params=pltpu.CompilerParams(
            collective_id=0, has_side_effects=True, vmem_limit_bytes=56 * 2**20
        ),
    )(
        charges,
        targets,
        panel_order,
        near_blocks,
        near_rows,
        near_cols,
        far_left,
        far_right,
        far_rows,
        far_slot,
        far_table,
    )


def solution(mesh):
    in_specs = (
        P(("groups", "rows"), None),
        P(("groups", "rows"), None),
        P(("groups", "rows"), None),
        P(("groups", "rows"), None, None),
        P(("groups", "rows")),
        P(("groups", "rows")),
        P(("groups", "rows"), None, None),
        P(("groups", "rows"), None, None),
        P(("groups", "rows")),
        P(("groups", "rows")),
        P(("groups", "rows"), None),
    )
    out_specs = (P(("groups", "rows"), None), P(("groups", "rows"), None))
    return jax.shard_map(shards, mesh=mesh, in_specs=in_specs, out_specs=out_specs, check_vma=False)
```

time: 131 us -> 57.8 us (0.44); the launches traced: 129 us -> 57.2 us
  Pallas kernels: 0 us -> 45.6 us
  local copies, waits for them, and re-layouts: 47.4 us -> 11 us
  starting transfers between devices: 35.7 us -> 0 us
  other arithmetic: 33.7 us -> 0 us
  matrix products: 6.8 us -> 0 us
  waiting for transfers between devices: 4.33 us -> 0 us
    pallas_call x0 -> x1, Pallas kernels: none -> 45.6 us  [shards(): pl.pallas_call(functools.partial(kernel, n), out_shape=(jax.ShapeDtypeStr...]
    all_to_all x2 -> x0, starting transfers between devices: 24.8 us -> none  [the longest x1 17.4 us: shards(): lax.all_to_all(slot_terms.reshape(row_devices, -1, excite).astype(jnp.bfl...]
    scatter-add x6 -> x0, other arithmetic: 22.6 us -> none  [the longest x1 7.06 us: shards(): back = back.at[safe_table].add(arrived)]
    gather x10 -> x0, local copies, waits for them, and re-layouts: 14.8 us -> none  [the longest x3 4.1 us: shards(): picked = local_blocks[safe_table]]
    ppermute x4 -> x0, starting transfers between devices: 10.9 us -> none  [the longest x2 7.09 us: extended_2(): before = lax.ppermute(last, axis, up)]
    reshape x7 -> x0, local copies, waits for them, and re-layouts: 9.67 us -> none  [the longest x2 5.76 us: shards(): arrived = arrived.reshape(slot_count, block_size, excite)]
    scatter x3 -> x0, local copies, waits for them, and re-layouts: 9.05 us -> none  [the longest x1 3.23 us: shards(): potentials = jnp.zeros((panel_total, excite), jnp.bfloat16).at[permute].s...]
    dot_general x4 -> x0, matrix products: 6.8 us -> none  [the longest x1 2.86 us: shards(): jnp.einsum('bij,bje->bie', near_blocks, extended[near_cols], preferred_el...]
  transfers between devices with their start and end apart: 6 -> 0, of which waited for: 2 -> 0; matrix products, arithmetic and copies ran while one was open for 24% -> 0% of each run, Pallas kernels for 0% -> 0%
where the time goes in v1:
time: 57.8 us; the launch traced here: 57.2 us
  Pallas kernels  45.6 us (79%)
  local copies, waits for them, and re-layouts  11 us (19%)
  between operations  0.64 us (1%)
    pallas_call x1, Pallas kernels, shards(): pl.pallas_call(functools.partial(kernel, n), out_shape=(jax.ShapeDtypeStr...  45.6 us
    unnamed x4, local copies, waits for them, and re-layouts  7.31 us
    pallas_call x2, local copies, waits for them, and re-layouts, shards(): pl.pallas_call(functools.partial(kernel, n), out_shape=(jax.ShapeDtypeStr...  3.66 us

profile of v1, /device:TPU:1, one launch (start us, length us, event | category | flops | bytes accessed | tf_op | source)
XLA Modules:
  0.0 57.2 jit_solution(5102736689650337070)
XLA Ops:
  0.6 1.7 %copy.13.charges = bf16[1024,64]{1,0:T(8,128)(2,1)} copy(bf16[1024,64]{0,1:T(8,128)(2,1)} %param.11) | data formatting | bytes 262144 | tf_op args[0]
  2.4 1.7 %copy.14.targets = bf16[1024,64]{1,0:T(8,128)(2,1)} copy(bf16[1024,64]{0,1:T(8,128)(2,1)} %param.12) | data formatting | bytes 262144 | tf_op args[1]
  4.1 1.9 %copy.15.fleft = bf16[16,128,32]{2,1,0:T(8,128)(2,1)} copy(bf16[16,128,32]{1,2,0:T(8,128)(2,1)} %param.17) | data formatting | bytes 262144 | tf_op args[6]
  6.0 1.9 %copy.16.fright = bf16[16,128,32]{2,1,0:T(8,128)(2,1)} copy(bf16[16,128,32]{1,2,0:T(8,128)(2,1)} %param.18) | data formatting | bytes 262144 | tf_op args[7]
  7.9 45.6 %shard_map.122 = (bf16[1024,64]{1,0:T(8,128)(2,1)}, f32[1024,64]{1,0:T(8,128)}) custom-call(bf16[1024,64]{1,0:T(8,128)(2,1)} %copy.13.charges, bf16[1024,64]{1,0:T(8,128)(2,1)} %copy.14.targets, s32[1,1024]{1,0:T(1,128)} %order.1, bf16[64,128,128]{2,1,0:T(8,128)(2,1)} %near_hbm.1, s32[64]{0:T(128)} %nrows.1, s32[64]{0:T(128)} %ncols.1, ...), custom_call_target="tpu_custom_call" | custom-call | tf_op jit(solution)/shard_map/pallas_call | solution.py:358
  53.6 1.7 %copy.17 = bf16[1024,64]{0,1:T(8,128)(2,1)} copy(bf16[1024,64]{1,0:T(8,128)(2,1)} %get-tuple-element.2) | data formatting | bytes 262144 | tf_op jit(solution)/shard_map/pallas_call | solution.py:358
  55.3 1.9 %copy.18 = f32[1024,64]{0,1:T(8,128)} copy(f32[1024,64]{1,0:T(8,128)} %get-tuple-element.3) | data formatting | bytes 524288 | tf_op jit(solution)/shard_map/pallas_call | solution.py:358

commit v2 on v1

--- a/solution.py
+++ b/solution.py
@@ -35,8 +35,8 @@
     pt,
     ext,
     want,
-    fr4,
-    fl4,
+    factors,
+    target,
     rslot,
     rin,
     lslot,
@@ -64,9 +64,9 @@
 ):
     me = lax.axis_index("rows")
     left, right = me - 1, me + 1
-    panels, exc = charges.shape
+    exc, panels = charges.shape
     nears, leaf, _ = near.shape
-    fars, _, rank = fleft.shape
+    fars, rank, _ = fleft.shape
     cap = ftable.shape[1] // n
     cl = panels // leaf
     wide = cap * rank
@@ -85,26 +85,11 @@
         )
 
     lane_slot = lax.broadcasted_iota(jnp.int32, (1, wide), 1) // rank
-    spread = (
-        lax.broadcasted_iota(jnp.int32, (rank, wide), 0)
-        == lax.broadcasted_iota(jnp.int32, (rank, wide), 1) % rank
-    ).astype(F32).astype(BF)
-    fr4[...] = dot(fright[...].reshape(fars * leaf, rank), spread, 1, 0).astype(BF).reshape(fars, leaf, wide)
-
-    def place(table, s):
-        slots = lane_slot + s * cap
-
-        def some(g, acc):
-            for k in range(16):
-                b = g * 16 + k
-                hot = (slots == fslot[b]).astype(F32).astype(BF)
-                acc = acc + table[b] * hot
-            return acc
-
-        zero = jnp.zeros((leaf, wide), BF)
-        if fars == 16:
-            return some(0, zero)
-        return lax.fori_loop(0, fars // 16, some, zero)
+    factors[:, :leaf] = fright[...].reshape(fars * rank, leaf)
+    factors[:, leaf:] = fleft[...].reshape(fars * rank, leaf)
+    for b in range(fars):
+        rank_lane = lax.broadcasted_iota(jnp.int32, (1, rank), 1)
+        target[:, b * rank : (b + 1) * rank] = fslot[b] * rank + rank_lane
 
     def send(src, dst, send_sem, recv_sem, d):
         return pltpu.make_async_remote_copy(
@@ -116,9 +101,13 @@
             device_id_type=pl.DeviceIdType.MESH,
         )
 
-    @pl.loop(0, n)
-    def _(s):
-        rslot[s] = place(fr4, s)
+    @pl.loop(0, n // GROUP)
+    def _(g):
+        shape = (GROUP * wide, fars * rank)
+        hot = lax.broadcasted_iota(jnp.int32, shape, 0) + g * (GROUP * wide) == target[...]
+        placed = dot(hot.astype(F32).astype(BF), factors[...], 1, 0).astype(BF)
+        rslot[pl.ds(g * GROUP, GROUP)] = placed[:, :leaf].reshape(GROUP, wide, leaf)
+        lslot[pl.ds(g * GROUP, GROUP)] = placed[:, leaf:].reshape(GROUP, wide, leaf)
 
     rin[me] = rslot[me]
     pl.semaphore_wait(barrier, n - 1)
@@ -131,8 +120,8 @@
     pt[...] = (
         lax.broadcasted_iota(jnp.int32, (panels, panels), 0) == order[...]
     ).astype(F32).astype(BF)
-    both = jnp.concatenate([charges[...], targets[...]], axis=1)
-    sorted_t = dot(both, pt[...], 0, 0).astype(BF)
+    both = jnp.concatenate([charges[...], targets[...]], axis=0)
+    sorted_t = dot(both, pt[...], 1, 0).astype(BF)
     for c in range(cl):
         ext[c + 1] = sorted_t[:exc, c * leaf : (c + 1) * leaf]
         want[pl.ds(c * exc, exc), :] = sorted_t[exc:, c * leaf : (c + 1) * leaf].astype(F32)
@@ -148,11 +137,8 @@
     def _():
         to_right.start()
 
-    fl4[...] = dot(fleft[...].reshape(fars * leaf, rank), spread, 1, 0).astype(BF).reshape(fars, leaf, wide)
-
     @pl.loop(0, n)
     def _(s):
-        lslot[s] = place(fl4, s)
         slots = lane_slot + s * cap
 
         def some(g, acc):
@@ -216,7 +202,7 @@
         )
 
     def coefs(t):
-        return chosen(dot(ext[1 : cl + 1].reshape(cl * exc, leaf), rin[t], 1, 0), owner_row(t))
+        return chosen(dot(ext[1 : cl + 1].reshape(cl * exc, leaf), rin[t], 1, 1), owner_row(t))
 
     cin[me] = coefs(me)
 
@@ -228,7 +214,7 @@
         send(cbuf.at[t], cin.at[me], c_send.at[d], c_recv.at[d], t).start()
 
     def far_out(s):
-        field[...] += dot(expanded(cin[s], rowtab[pl.ds(s, 1), :]), lslot[s], 1, 1)
+        field[...] += dot(expanded(cin[s], rowtab[pl.ds(s, 1), :]), lslot[s], 1, 0)
 
     far_out(me)
 
@@ -241,7 +227,7 @@
     misfit[...] = (field[...] - want[...]).astype(BF).reshape(misfit.shape)
 
     def adjoint(s):
-        product = dot(misfit[...].reshape(cl * exc, leaf), lslot[s], 1, 0)
+        product = dot(misfit[...].reshape(cl * exc, leaf), lslot[s], 1, 1)
         return chosen(product, rowtab[pl.ds(s, 1), :])
 
     @pl.loop(1, n)
@@ -279,7 +265,7 @@
     inner = pl.ds(exc, cl * exc)
 
     def far_back(t):
-        back[inner, :] += dot(expanded(ain[t], owner_row(t)), rin[t], 1, 1)
+        back[inner, :] += dot(expanded(ain[t], owner_row(t)), rin[t], 1, 0)
 
     far_back(me)
 
@@ -308,9 +294,9 @@
     mid = rest.astype(BF)
     low = (rest - mid.astype(F32)).astype(BF)
     parts = jnp.concatenate([high, mid, flat(field[...]).astype(BF), low], axis=0)
-    result = dot(pt[...], parts, 1, 1)
-    pot[...] = result[:, 2 * exc : 3 * exc].astype(BF)
-    grad[...] = (result[:, exc : 2 * exc] + result[:, 3 * exc :]) + result[:, :exc]
+    result = dot(parts, pt[...], 1, 1)
+    pot[...] = result[2 * exc : 3 * exc].astype(BF)
+    grad[...] = (result[exc : 2 * exc] + result[3 * exc :]) + result[:exc]
 
     @pl.loop(1, n)
     def _(d):
@@ -355,11 +341,11 @@
     anywhere = pl.BlockSpec(memory_space=pl.ANY)
     sems = pltpu.SemaphoreType.DMA((n,))
     pair = pltpu.SemaphoreType.DMA((2,))
-    return pl.pallas_call(
+    potentials, gradient = pl.pallas_call(
         functools.partial(kernel, n),
         out_shape=(
-            jax.ShapeDtypeStruct((panels, exc), BF),
-            jax.ShapeDtypeStruct((panels, exc), F32),
+            jax.ShapeDtypeStruct((exc, panels), BF),
+            jax.ShapeDtypeStruct((exc, panels), F32),
         ),
         in_specs=[vmem, vmem, vmem, anywhere, smem, smem, vmem, vmem, smem, smem, smem],
         out_specs=(vmem, vmem),
@@ -368,11 +354,11 @@
             pltpu.VMEM((panels, panels), BF),
             pltpu.VMEM((cl + 2, exc, leaf), BF),
             pltpu.VMEM((cl * exc, leaf), F32),
-            pltpu.VMEM((fars, leaf, wide), BF),
-            pltpu.VMEM((fars, leaf, wide), BF),
-            pltpu.VMEM((n, leaf, wide), BF),
-            pltpu.VMEM((n, leaf, wide), BF),
-            pltpu.VMEM((n, leaf, wide), BF),
+            pltpu.VMEM((fars * rank, 2 * leaf), BF),
+            pltpu.VMEM((1, fars * rank), jnp.int32),
+            pltpu.VMEM((n, wide, leaf), BF),
+            pltpu.VMEM((n, wide, leaf), BF),
+            pltpu.VMEM((n, wide, leaf), BF),
             pltpu.VMEM((n, exc, wide), BF),
             pltpu.VMEM((n, exc, wide), BF),
             pltpu.VMEM((n, exc, wide), BF),
@@ -399,18 +385,19 @@
             collective_id=0, has_side_effects=True, vmem_limit_bytes=56 * 2**20
         ),
     )(
-        charges,
-        targets,
+        charges.T,
+        targets.T,
         panel_order,
         near_blocks,
         near_rows,
         near_cols,
-        far_left,
-        far_right,
+        far_left.transpose(0, 2, 1),
+        far_right.transpose(0, 2, 1),
         far_rows,
         far_slot,
         far_table,
     )
+    return potentials.T, gradient.T
 
 
 def solution(mesh):

time: 57.8 us -> 50.6 us (0.88)
  local copies, waits for them, and re-layouts: 11 us -> 3.24 us
  Pallas kernels: 45.6 us -> 46.2 us
    unnamed x4 -> x2, local copies, waits for them, and re-layouts: 7.31 us -> 3.24 us
    pallas_call x2 -> x0, local copies, waits for them, and re-layouts: 3.66 us -> none  [shards(): pl.pallas_call(functools.partial(kernel, n), out_shape=(jax.ShapeDtypeStr...]
    pallas_call x1, Pallas kernels: 45.6 us -> 46.2 us  [shards(): pl.pallas_call(functools.partial(kernel, n), out_shape=(jax.ShapeDtypeStr...]
where the time goes in v2:
time: 50.6 us; the launch traced here: 50.1 us
  Pallas kernels  46.2 us (91%)
  local copies, waits for them, and re-layouts  3.24 us (6%)
  between operations  0.64 us (1%)
    pallas_call x1, Pallas kernels, shards(): pl.pallas_call(functools.partial(kernel, n), out_shape=(jax.ShapeDtypeStr...  46.2 us
    unnamed x2, local copies, waits for them, and re-layouts  3.24 us

profile of v2, /device:TPU:1, one launch (start us, length us, event | category | flops | bytes accessed | tf_op | source)
XLA Modules:
  0.0 50.1 jit_solution(5944421702193640829)
XLA Ops:
  0.6 46.2 %shard_map.122 = (bf16[64,1024]{1,0:T(8,128)(2,1)}, f32[64,1024]{1,0:T(8,128)}) custom-call(bf16[64,1024]{1,0:T(8,128)(2,1)} %bitcast.7, bf16[64,1024]{1,0:T(8,128)(2,1)} %bitcast.8, s32[1,1024]{1,0:T(1,128)} %order.1, bf16[64,128,128]{2,1,0:T(8,128)(2,1)} %near_hbm.1, s32[64]{0:T(128)} %nrows.1, s32[64]{0:T(128)} %ncols.1, bf16[16,32,128]{2,1,0:T(8,128)(2,1)} %bitcast.9, ...), custom_call_target="tpu_custom_call" | custom-call | tf_op jit(solution)/shard_map/pallas_call | solution.py:344
  46.9 1.6 %copy.15 = bf16[1024,64]{0,1:T(8,128)(2,1)} copy(bf16[1024,64]{0,1:T(8,128)(2,1)} %bitcast.11) | data formatting | bytes 262144
  48.4 1.7 %copy.16 = f32[1024,64]{0,1:T(8,128)} copy(f32[1024,64]{0,1:T(8,128)} %bitcast.6) | data formatting | bytes 524288

commit v3 on v2

--- a/solution.py
+++ b/solution.py
@@ -33,6 +33,7 @@
     grad,
     near,
     pt,
+    inverse,
     ext,
     want,
     factors,
@@ -112,10 +113,40 @@
     rin[me] = rslot[me]
     pl.semaphore_wait(barrier, n - 1)
 
-    @pl.loop(1, n)
-    def _(d):
-        t = lax.rem(me + d, n)
-        send(rslot.at[t], rin.at[me], r_send.at[d], r_recv.at[d], t).start()
+    groups = n // GROUP
+
+    def each(first, act):
+        for k in range(GROUP):
+            other = first + lax.rem(me + k, GROUP)
+
+            @pl.when(other != me)
+            def _():
+                act(other)
+
+    def group_at(g):
+        return lax.rem(me // GROUP + g, groups) * GROUP
+
+    def r_copy(t):
+        return send(rslot.at[t], rin.at[me], r_send.at[t], r_recv.at[me], t)
+
+    def r_arrival(t):
+        return send(rslot.at[me], rin.at[t], r_send.at[t], r_recv.at[t], t)
+
+    def c_copy(t):
+        return send(cbuf.at[t], cin.at[me], c_send.at[t], c_recv.at[me], t)
+
+    def c_arrival(t):
+        return send(cbuf.at[t], cin.at[t], c_send.at[t], c_recv.at[t], t)
+
+    def a_copy(t):
+        return send(abuf.at[t], ain.at[me], a_send.at[t], a_recv.at[me], t)
+
+    def a_arrival(t):
+        return send(abuf.at[t], ain.at[t], a_send.at[t], a_recv.at[t], t)
+
+    @pl.loop(0, groups)
+    def _(g):
+        each(group_at(g), lambda t: r_copy(t).start())
 
     pt[...] = (
         lax.broadcasted_iota(jnp.int32, (panels, panels), 0) == order[...]
@@ -147,7 +178,7 @@
                 acc = jnp.where(slots == fslot[b], frows[b], acc)
             return acc
 
-        rowtab[pl.ds(s, 1), :] = lax.fori_loop(0, fars // 16, some, jnp.zeros((1, wide), jnp.int32))
+        rowtab[s // GROUP, pl.ds(lax.rem(s, GROUP), 1)] = lax.fori_loop(0, fars // 16, some, jnp.zeros((1, wide), jnp.int32))
 
     @pl.when(me < n - 1)
     def _():
@@ -184,59 +215,64 @@
             blocks.append(near[b])
         field[...] += dot(jnp.concatenate(ins, axis=1), jnp.concatenate(blocks, axis=1), 1, 1)
 
-    def owner_row(t):
-        row = jnp.full((1, wide), -1, jnp.int32)
-        for k in range(cap):
-            row = jnp.where(lane_slot == k, ftable[0, t * cap + k], row)
-        return row
-
-    def chosen(product, row):
-        total = jnp.zeros((exc, wide), F32)
+    def owner_row(first):
+        rows = []
+        for t in range(GROUP):
+            row = jnp.full((1, wide), -1, jnp.int32)
+            for k in range(cap):
+                row = jnp.where(lane_slot == k, ftable[0, (first + t) * cap + k], row)
+            rows.append(row)
+        return jnp.concatenate(rows, axis=1)
+
+    def target_row(first):
+        return jnp.concatenate([rowtab[first // GROUP, t : t + 1] for t in range(GROUP)], axis=1)
+
+    def chosen(value, factor, row, out, first):
+        product = dot(value, factor[pl.ds(first, GROUP)].reshape(GROUP * wide, leaf), 1, 1)
+        total = jnp.zeros((exc, GROUP * wide), F32)
         for c in range(cl):
             total = total + jnp.where(row == c, product[c * exc : (c + 1) * exc], 0.0)
-        return total.astype(BF)
-
-    def expanded(value, row):
-        return jnp.concatenate(
-            [value * (row == c).astype(F32).astype(BF) for c in range(cl)], axis=0
-        )
-
-    def coefs(t):
-        return chosen(dot(ext[1 : cl + 1].reshape(cl * exc, leaf), rin[t], 1, 1), owner_row(t))
-
-    cin[me] = coefs(me)
-
-    @pl.loop(1, n)
-    def _(d):
-        t = lax.rem(me + n - d, n)
-        send(rslot.at[me], rin.at[t], r_send.at[d], r_recv.at[d], t).wait_recv()
-        cbuf[t] = coefs(t)
-        send(cbuf.at[t], cin.at[me], c_send.at[d], c_recv.at[d], t).start()
-
-    def far_out(s):
-        field[...] += dot(expanded(cin[s], rowtab[pl.ds(s, 1), :]), lslot[s], 1, 0)
-
-    far_out(me)
-
-    @pl.loop(1, n)
-    def _(d):
-        s = lax.rem(me + d, n)
-        send(cbuf.at[s], cin.at[s], c_send.at[d], c_recv.at[d], s).wait_recv()
-        far_out(s)
+        total = total.astype(BF)
+        for t in range(GROUP):
+            out[first + t] = total[:, t * wide : (t + 1) * wide]
+
+    def expanded(value, row, factor, first):
+        parts = jnp.concatenate([value[first + t] for t in range(GROUP)], axis=1)
+        masks = [(row == c).astype(F32).astype(BF) for c in range(cl)]
+        spread = jnp.concatenate([parts * mask for mask in masks], axis=0)
+        return dot(spread, factor[pl.ds(first, GROUP)].reshape(GROUP * wide, leaf), 1, 0)
+
+    mine = ext[1 : cl + 1].reshape(cl * exc, leaf)
+
+    @pl.loop(0, groups)
+    def _(g):
+        first = group_at(groups - g)
+        each(first, lambda t: r_arrival(t).wait_recv())
+        chosen(mine, rin, owner_row(first), cbuf, first)
+        each(first, lambda t: c_copy(t).start())
+
+    cin[me] = cbuf[me]
+
+    order_rows = jnp.broadcast_to(order[...].astype(F32), (8, panels))
+    spot = jnp.transpose(order_rows)[:, :1]
+    lanes = lax.broadcasted_iota(jnp.int32, (panels, panels), 1).astype(F32)
+    inverse[...] = (lanes == spot).astype(F32).astype(BF)
+
+    @pl.loop(0, groups)
+    def _(g):
+        first = group_at(g)
+        each(first, lambda t: c_arrival(t).wait_recv())
+        field[...] += expanded(cin, target_row(first), lslot, first)
 
     misfit[...] = (field[...] - want[...]).astype(BF).reshape(misfit.shape)
 
-    def adjoint(s):
-        product = dot(misfit[...].reshape(cl * exc, leaf), lslot[s], 1, 1)
-        return chosen(product, rowtab[pl.ds(s, 1), :])
-
-    @pl.loop(1, n)
-    def _(d):
-        s = lax.rem(me + d, n)
-        abuf[s] = adjoint(s)
-        send(abuf.at[s], ain.at[me], a_send.at[d], a_recv.at[d], s).start()
-
-    ain[me] = adjoint(me)
+    @pl.loop(0, groups)
+    def _(g):
+        first = group_at(g)
+        chosen(misfit[...].reshape(cl * exc, leaf), lslot, target_row(first), abuf, first)
+        each(first, lambda t: a_copy(t).start())
+
+    ain[me] = abuf[me]
 
     back[...] = jnp.zeros(back.shape, F32)
 
@@ -264,16 +300,11 @@
 
     inner = pl.ds(exc, cl * exc)
 
-    def far_back(t):
-        back[inner, :] += dot(expanded(ain[t], owner_row(t)), rin[t], 1, 0)
-
-    far_back(me)
-
-    @pl.loop(1, n)
-    def _(d):
-        t = lax.rem(me + n - d, n)
-        send(abuf.at[t], ain.at[t], a_send.at[d], a_recv.at[d], t).wait_recv()
-        far_back(t)
+    @pl.loop(0, groups)
+    def _(g):
+        first = group_at(groups - g)
+        each(first, lambda t: a_arrival(t).wait_recv())
+        back[inner, :] += expanded(ain, owner_row(first), rin, first)
 
     @pl.when(me < n - 1)
     def _():
@@ -294,17 +325,16 @@
     mid = rest.astype(BF)
     low = (rest - mid.astype(F32)).astype(BF)
     parts = jnp.concatenate([high, mid, flat(field[...]).astype(BF), low], axis=0)
-    result = dot(parts, pt[...], 1, 1)
+    result = dot(parts, inverse[...], 1, 0)
     pot[...] = result[2 * exc : 3 * exc].astype(BF)
     grad[...] = (result[exc : 2 * exc] + result[3 * exc :]) + result[:exc]
 
-    @pl.loop(1, n)
-    def _(d):
-        t = lax.rem(me + d, n)
-        s = lax.rem(me + n - d, n)
-        send(rslot.at[t], rin.at[me], r_send.at[d], r_recv.at[d], t).wait_send()
-        send(cbuf.at[s], cin.at[me], c_send.at[d], c_recv.at[d], s).wait_send()
-        send(abuf.at[t], ain.at[me], a_send.at[d], a_recv.at[d], t).wait_send()
+    @pl.loop(0, groups)
+    def _(g):
+        first = group_at(g)
+        each(first, lambda t: r_copy(t).wait_send())
+        each(first, lambda t: c_copy(t).wait_send())
+        each(first, lambda t: a_copy(t).wait_send())
 
     @pl.when(me > 0)
     def _():
@@ -352,6 +382,7 @@
         scratch_shapes=[
             pltpu.VMEM((nears, leaf, leaf), BF),
             pltpu.VMEM((panels, panels), BF),
+            pltpu.VMEM((panels, panels), BF),
             pltpu.VMEM((cl + 2, exc, leaf), BF),
             pltpu.VMEM((cl * exc, leaf), F32),
             pltpu.VMEM((fars * rank, 2 * leaf), BF),
@@ -368,7 +399,7 @@
             pltpu.VMEM(((cl + 2) * exc, leaf), F32),
             pltpu.VMEM((2, exc, leaf), BF),
             pltpu.VMEM((2, exc, leaf), BF),
-            pltpu.VMEM((n, wide), jnp.int32),
+            pltpu.VMEM((n // GROUP, GROUP, wide), jnp.int32),
             pltpu.SemaphoreType.DMA,
             sems,
             sems,

time: 50.6 us -> 46.6 us (0.921)
  Pallas kernels: 46.2 us -> 42.5 us
    pallas_call x1, Pallas kernels: 46.2 us -> 42.5 us  [shards(): pl.pallas_call(functools.partial(kernel, n), out_shape=(jax.ShapeDtypeStr...]
where the time goes in v3:
time: 46.6 us; the launch traced here: 46.4 us
  Pallas kernels  42.5 us (91%)
  local copies, waits for them, and re-layouts  3.24 us (7%)
  between operations  0.64 us (1%)
    pallas_call x1, Pallas kernels, shards(): pl.pallas_call(functools.partial(kernel, n), out_shape=(jax.ShapeDtypeStr...  42.5 us
    unnamed x2, local copies, waits for them, and re-layouts  3.24 us

profile of v3, /device:TPU:1, one launch (start us, length us, event | category | flops | bytes accessed | tf_op | source)
XLA Modules:
  0.0 46.4 jit_solution(17418508366361430394)
XLA Ops:
  0.6 42.5 %shard_map.122 = (bf16[64,1024]{1,0:T(8,128)(2,1)}, f32[64,1024]{1,0:T(8,128)}) custom-call(bf16[64,1024]{1,0:T(8,128)(2,1)} %bitcast.7, bf16[64,1024]{1,0:T(8,128)(2,1)} %bitcast.8, s32[1,1024]{1,0:T(1,128)} %order.1, bf16[64,128,128]{2,1,0:T(8,128)(2,1)} %near_hbm.1, s32[64]{0:T(128)} %nrows.1, s32[64]{0:T(128)} %ncols.1, bf16[16,32,128]{2,1,0:T(8,128)(2,1)} %bitcast.9, ...), custom_call_target="tpu_custom_call" | custom-call | tf_op jit(solution)/shard_map/pallas_call | solution.py:374
  43.1 1.6 %copy.15 = bf16[1024,64]{0,1:T(8,128)(2,1)} copy(bf16[1024,64]{0,1:T(8,128)(2,1)} %bitcast.11) | data formatting | bytes 262144
  44.7 1.7 %copy.16 = f32[1024,64]{0,1:T(8,128)} copy(f32[1024,64]{0,1:T(8,128)} %bitcast.6) | data formatting | bytes 524288

commit v4 on v3

--- a/solution.py
+++ b/solution.py
@@ -29,11 +29,9 @@
     frows,
     fslot,
     ftable,
-    pot,
-    grad,
+    parts,
     near,
     pt,
-    inverse,
     ext,
     want,
     factors,
@@ -48,6 +46,7 @@
     field,
     misfit,
     back,
+    rim,
     rimbuf,
     rimin,
     rowtab,
@@ -253,11 +252,6 @@
 
     cin[me] = cbuf[me]
 
-    order_rows = jnp.broadcast_to(order[...].astype(F32), (8, panels))
-    spot = jnp.transpose(order_rows)[:, :1]
-    lanes = lax.broadcasted_iota(jnp.int32, (panels, panels), 1).astype(F32)
-    inverse[...] = (lanes == spot).astype(F32).astype(BF)
-
     @pl.loop(0, groups)
     def _(g):
         first = group_at(g)
@@ -274,19 +268,25 @@
 
     ain[me] = abuf[me]
 
-    back[...] = jnp.zeros(back.shape, F32)
+    rim[...] = jnp.zeros(rim.shape, F32)
+
+    def near_back(g, columns):
+        ins = []
+        for k in range(GROUP):
+            b = g * GROUP + k
+            value, col = misfit[nrows[b]], ncols[b]
+            ins.append(
+                jnp.concatenate([lax.select(col == c, value, nothing) for c in columns], axis=0)
+            )
+        blocks = near[pl.ds(g * GROUP, GROUP)].reshape(GROUP * leaf, leaf)
+        return dot(jnp.concatenate(ins, axis=1), blocks, 1, 0)
 
     @pl.loop(0, nears // GROUP)
     def _(g):
-        ins = [
-            stacked(misfit[nrows[g * GROUP + k]], ncols[g * GROUP + k], cl + 2)
-            for k in range(GROUP)
-        ]
-        blocks = near[pl.ds(g * GROUP, GROUP)].reshape(GROUP * leaf, leaf)
-        back[...] += dot(jnp.concatenate(ins, axis=1), blocks, 1, 0)
-
-    rimbuf[0] = back[:exc].astype(BF)
-    rimbuf[1] = back[(cl + 1) * exc :].astype(BF)
+        rim[...] += near_back(g, (0, cl + 1))
+
+    rimbuf[0] = rim[:exc].astype(BF)
+    rimbuf[1] = rim[exc:].astype(BF)
     rim_left = send(rimbuf.at[0], rimin.at[1], b_send.at[0], b_recv.at[0], left)
     rim_right = send(rimbuf.at[1], rimin.at[0], b_send.at[1], b_recv.at[1], right)
 
@@ -298,36 +298,38 @@
     def _():
         rim_right.start()
 
-    inner = pl.ds(exc, cl * exc)
+    back[...] = jnp.zeros(back.shape, F32)
+
+    @pl.loop(0, nears // GROUP)
+    def _(g):
+        back[...] += near_back(g, range(1, cl + 1))
+
 
     @pl.loop(0, groups)
     def _(g):
         first = group_at(groups - g)
         each(first, lambda t: a_arrival(t).wait_recv())
-        back[inner, :] += expanded(ain, owner_row(first), rin, first)
+        back[...] += expanded(ain, owner_row(first), rin, first)
 
     @pl.when(me < n - 1)
     def _():
         rim_left.wait_recv()
-        back[pl.ds(cl * exc, exc), :] += rimin[1].astype(F32)
+        back[pl.ds((cl - 1) * exc, exc), :] += rimin[1].astype(F32)
 
     @pl.when(me > 0)
     def _():
         rim_right.wait_recv()
-        back[pl.ds(exc, exc), :] += rimin[0].astype(F32)
+        back[pl.ds(0, exc), :] += rimin[0].astype(F32)
 
     def flat(value):
         return jnp.concatenate([value[c * exc : (c + 1) * exc] for c in range(cl)], axis=1)
 
-    full = flat(back[inner, :])
+    full = flat(back[...])
     high = full.astype(BF)
     rest = full - high.astype(F32)
     mid = rest.astype(BF)
     low = (rest - mid.astype(F32)).astype(BF)
-    parts = jnp.concatenate([high, mid, flat(field[...]).astype(BF), low], axis=0)
-    result = dot(parts, inverse[...], 1, 0)
-    pot[...] = result[2 * exc : 3 * exc].astype(BF)
-    grad[...] = (result[exc : 2 * exc] + result[3 * exc :]) + result[:exc]
+    parts[...] = jnp.concatenate([high, mid, flat(field[...]).astype(BF), low], axis=0)
 
     @pl.loop(0, groups)
     def _(g):
@@ -345,6 +347,16 @@
     def _():
         to_right.wait_send()
         rim_right.wait_send()
+
+
+def unsort(order, parts, pot, grad):
+    exc, panels = pot.shape
+    spot = jnp.transpose(jnp.broadcast_to(order[...].astype(F32), (8, panels)))[:, :1]
+    lanes = lax.broadcasted_iota(jnp.int32, (panels, panels), 1).astype(F32)
+    inverse = (lanes == spot).astype(F32).astype(BF)
+    result = dot(parts[...], inverse, 1, 0)
+    pot[...] = result[2 * exc : 3 * exc].astype(BF)
+    grad[...] = (result[exc : 2 * exc] + result[3 * exc :]) + result[:exc]
 
 
 def shards(
@@ -371,17 +383,13 @@
     anywhere = pl.BlockSpec(memory_space=pl.ANY)
     sems = pltpu.SemaphoreType.DMA((n,))
     pair = pltpu.SemaphoreType.DMA((2,))
-    potentials, gradient = pl.pallas_call(
+    parts = pl.pallas_call(
         functools.partial(kernel, n),
-        out_shape=(
-            jax.ShapeDtypeStruct((exc, panels), BF),
-            jax.ShapeDtypeStruct((exc, panels), F32),
-        ),
+        out_shape=jax.ShapeDtypeStruct((4 * exc, panels), BF),
         in_specs=[vmem, vmem, vmem, anywhere, smem, smem, vmem, vmem, smem, smem, smem],
-        out_specs=(vmem, vmem),
+        out_specs=vmem,
         scratch_shapes=[
             pltpu.VMEM((nears, leaf, leaf), BF),
-            pltpu.VMEM((panels, panels), BF),
             pltpu.VMEM((panels, panels), BF),
             pltpu.VMEM((cl + 2, exc, leaf), BF),
             pltpu.VMEM((cl * exc, leaf), F32),
@@ -396,7 +404,8 @@
             pltpu.VMEM((n, exc, wide), BF),
             pltpu.VMEM((cl * exc, leaf), F32),
             pltpu.VMEM((cl, exc, leaf), BF),
-            pltpu.VMEM(((cl + 2) * exc, leaf), F32),
+            pltpu.VMEM((cl * exc, leaf), F32),
+            pltpu.VMEM((2 * exc, leaf), F32),
             pltpu.VMEM((2, exc, leaf), BF),
             pltpu.VMEM((2, exc, leaf), BF),
             pltpu.VMEM((n // GROUP, GROUP, wide), jnp.int32),
@@ -428,6 +437,16 @@
         far_slot,
         far_table,
     )
+    potentials, gradient = pl.pallas_call(
+        unsort,
+        out_shape=(
+            jax.ShapeDtypeStruct((exc, panels), BF),
+            jax.ShapeDtypeStruct((exc, panels), F32),
+        ),
+        in_specs=[vmem, vmem],
+        out_specs=(vmem, vmem),
+        compiler_params=pltpu.CompilerParams(vmem_limit_bytes=32 * 2**20),
+    )(panel_order, parts)
     return potentials.T, gradient.T
 
 

time: 46.6 us -> 46.8 us (level)
  Pallas kernels: 42.5 us -> 44.9 us
  local copies, waits for them, and re-layouts: 3.24 us -> 1.04 us
    pallas_call x1 -> x2, Pallas kernels: 42.5 us -> 44.9 us  [the longest x1 43 us: shards(): pl.pallas_call(functools.partial(kernel, n), out_shape=jax.ShapeDtypeStru...]
    unnamed x2 -> x4, local copies, waits for them, and re-layouts: 3.24 us -> 1.04 us
where the time goes in v4:
time: 46.8 us; the launch traced here: 46.6 us
  Pallas kernels  44.9 us (96%)
  local copies, waits for them, and re-layouts  1.04 us (2%)
  between operations  0.67 us (1%)
    pallas_call x1, Pallas kernels, shards(): pl.pallas_call(functools.partial(kernel, n), out_shape=jax.ShapeDtypeStru...  43 us
    pallas_call x1, Pallas kernels, shards(): pl.pallas_call(unsort, out_shape=(jax.ShapeDtypeStruct((exc, panels), BF)...  1.87 us
    unnamed x4, local copies, waits for them, and re-layouts  1.04 us

profile of v4, /device:TPU:1, one launch (start us, length us, event | category | flops | bytes accessed | tf_op | source)
XLA Modules:
  0.0 46.6 jit_solution(5423144938041742156)
XLA Ops:
  0.6 0.0 copy-start.1
  0.6 43.0 %shard_map.122.parts = bf16[256,1024]{1,0:T(8,128)(2,1)} custom-call(bf16[64,1024]{1,0:T(8,128)(2,1)} %bitcast.6, bf16[64,1024]{1,0:T(8,128)(2,1)} %bitcast.7, s32[1,1024]{1,0:T(1,128)} %order.3, bf16[64,128,128]{2,1,0:T(8,128)(2,1)} %near_hbm.1, s32[64]{0:T(128)} %nrows.1, s32[64]{0:T(128)} %ncols.1, bf16[16,32,128]{2,1,0:T(8,128)(2,1)} %bitcast.8, ...), custom_call_target="tpu_custom_call" | custom-call | tf_op jit(solution)/shard_map/pallas_call | solution.py:386
  43.7 0.0 copy-done.1
  43.7 0.0 copy-start
  43.7 1.0 %copy-done = bf16[256,1024]{1,0:T(8,128)(2,1)S(1)} copy-done((bf16[256,1024]{1,0:T(8,128)(2,1)S(1)}, bf16[256,1024]{1,0:T(8,128)(2,1)}, u32[]{:S(2)}) %copy-start) | copy-done | bytes 524312
  44.7 1.9 %shard_map.123 = (bf16[64,1024]{1,0:T(8,128)(2,1)}, f32[64,1024]{1,0:T(8,128)}) custom-call(s32[1,1024]{1,0:T(1,128)S(1)} %copy-done.1, bf16[256,1024]{1,0:T(8,128)(2,1)S(1)} %copy-done), custom_call_target="tpu_custom_call" | custom-call | tf_op jit(solution)/shard_map/pallas_call | solution.py:440
Async XLA Ops:
  0.6 43.0 %copy-start.1 = (s32[1,1024]{1,0:T(1,128)S(1)}, s32[1,1024]{1,0:T(1,128)}, u32[]{:S(2)}) copy-start(s32[1,1024]{1,0:T(1,128)} %order.3) | copy-start | bytes 12292
  43.7 1.0 %copy-start = (bf16[256,1024]{1,0:T(8,128)(2,1)S(1)}, bf16[256,1024]{1,0:T(8,128)(2,1)}, u32[]{:S(2)}) copy-start(bf16[256,1024]{1,0:T(8,128)(2,1)} %shard_map.122.parts) | copy-start | bytes 1572868

commit v5 on v4

--- a/solution.py
+++ b/solution.py
@@ -10,6 +10,7 @@
 BF = jnp.bfloat16
 F32 = jnp.float32
 GROUP = 4
+NEAR_GROUP = 16
 
 
 def dot(a, b, ca, cb):
@@ -46,7 +47,6 @@
     field,
     misfit,
     back,
-    rim,
     rimbuf,
     rimin,
     rowtab,
@@ -205,11 +205,11 @@
 
     field[...] = jnp.zeros(field.shape, F32)
 
-    @pl.loop(0, nears // GROUP)
+    @pl.loop(0, nears // NEAR_GROUP)
     def _(g):
         ins, blocks = [], []
-        for k in range(GROUP):
-            b = g * GROUP + k
+        for k in range(NEAR_GROUP):
+            b = g * NEAR_GROUP + k
             ins.append(stacked(ext[ncols[b]], nrows[b], cl))
             blocks.append(near[b])
         field[...] += dot(jnp.concatenate(ins, axis=1), jnp.concatenate(blocks, axis=1), 1, 1)
@@ -268,25 +268,19 @@
 
     ain[me] = abuf[me]
 
-    rim[...] = jnp.zeros(rim.shape, F32)
-
-    def near_back(g, columns):
-        ins = []
-        for k in range(GROUP):
-            b = g * GROUP + k
-            value, col = misfit[nrows[b]], ncols[b]
-            ins.append(
-                jnp.concatenate([lax.select(col == c, value, nothing) for c in columns], axis=0)
-            )
-        blocks = near[pl.ds(g * GROUP, GROUP)].reshape(GROUP * leaf, leaf)
-        return dot(jnp.concatenate(ins, axis=1), blocks, 1, 0)
-
-    @pl.loop(0, nears // GROUP)
-    def _(g):
-        rim[...] += near_back(g, (0, cl + 1))
-
-    rimbuf[0] = rim[:exc].astype(BF)
-    rimbuf[1] = rim[exc:].astype(BF)
+    back[...] = jnp.zeros(back.shape, F32)
+
+    @pl.loop(0, nears // NEAR_GROUP)
+    def _(g):
+        ins = [
+            stacked(misfit[nrows[g * NEAR_GROUP + k]], ncols[g * NEAR_GROUP + k], cl + 2)
+            for k in range(NEAR_GROUP)
+        ]
+        blocks = near[pl.ds(g * NEAR_GROUP, NEAR_GROUP)].reshape(NEAR_GROUP * leaf, leaf)
+        back[...] += dot(jnp.concatenate(ins, axis=1), blocks, 1, 0)
+
+    rimbuf[0] = back[:exc].astype(BF)
+    rimbuf[1] = back[(cl + 1) * exc :].astype(BF)
     rim_left = send(rimbuf.at[0], rimin.at[1], b_send.at[0], b_recv.at[0], left)
     rim_right = send(rimbuf.at[1], rimin.at[0], b_send.at[1], b_recv.at[1], right)
 
@@ -298,33 +292,28 @@
     def _():
         rim_right.start()
 
-    back[...] = jnp.zeros(back.shape, F32)
-
-    @pl.loop(0, nears // GROUP)
-    def _(g):
-        back[...] += near_back(g, range(1, cl + 1))
-
+    inner = pl.ds(exc, cl * exc)
 
     @pl.loop(0, groups)
     def _(g):
         first = group_at(groups - g)
         each(first, lambda t: a_arrival(t).wait_recv())
-        back[...] += expanded(ain, owner_row(first), rin, first)
+        back[inner, :] += expanded(ain, owner_row(first), rin, first)
 
     @pl.when(me < n - 1)
     def _():
         rim_left.wait_recv()
-        back[pl.ds((cl - 1) * exc, exc), :] += rimin[1].astype(F32)
+        back[pl.ds(cl * exc, exc), :] += rimin[1].astype(F32)
 
     @pl.when(me > 0)
     def _():
         rim_right.wait_recv()
-        back[pl.ds(0, exc), :] += rimin[0].astype(F32)
+        back[pl.ds(exc, exc), :] += rimin[0].astype(F32)
 
     def flat(value):
         return jnp.concatenate([value[c * exc : (c + 1) * exc] for c in range(cl)], axis=1)
 
-    full = flat(back[...])
+    full = flat(back[inner, :])
     high = full.astype(BF)
     rest = full - high.astype(F32)
     mid = rest.astype(BF)
@@ -404,8 +393,7 @@
             pltpu.VMEM((n, exc, wide), BF),
             pltpu.VMEM((cl * exc, leaf), F32),
             pltpu.VMEM((cl, exc, leaf), BF),
-            pltpu.VMEM((cl * exc, leaf), F32),
-            pltpu.VMEM((2 * exc, leaf), F32),
+            pltpu.VMEM(((cl + 2) * exc, leaf), F32),
             pltpu.VMEM((2, exc, leaf), BF),
             pltpu.VMEM((2, exc, leaf), BF),
             pltpu.VMEM((n // GROUP, GROUP, wide), jnp.int32),

time: 46.8 us -> 43.1 us (0.921)
  Pallas kernels: 44.9 us -> 41.2 us
    pallas_call x1, Pallas kernels: 43 us -> 39.3 us  [shards(): pl.pallas_call(functools.partial(kernel, n), out_shape=jax.ShapeDtypeStru...]
where the time goes in v5:
time: 43.1 us; the launch traced here: 42.9 us
  Pallas kernels  41.2 us (96%)
  local copies, waits for them, and re-layouts  1.04 us (2%)
  between operations  0.67 us (2%)
    pallas_call x1, Pallas kernels, shards(): pl.pallas_call(functools.partial(kernel, n), out_shape=jax.ShapeDtypeStru...  39.3 us
    pallas_call x1, Pallas kernels, shards(): pl.pallas_call(unsort, out_shape=(jax.ShapeDtypeStruct((exc, panels), BF)...  1.88 us
    unnamed x4, local copies, waits for them, and re-layouts  1.04 us

profile of v5, /device:TPU:1, one launch (start us, length us, event | category | flops | bytes accessed | tf_op | source)
XLA Modules:
  0.0 42.9 jit_solution(10247721817280813933)
XLA Ops:
  0.6 0.0 copy-start.1
  0.6 39.3 %shard_map.122.parts = bf16[256,1024]{1,0:T(8,128)(2,1)} custom-call(bf16[64,1024]{1,0:T(8,128)(2,1)} %bitcast.6, bf16[64,1024]{1,0:T(8,128)(2,1)} %bitcast.7, s32[1,1024]{1,0:T(1,128)} %order.3, bf16[64,128,128]{2,1,0:T(8,128)(2,1)} %near_hbm.1, s32[64]{0:T(128)} %nrows.1, s32[64]{0:T(128)} %ncols.1, bf16[16,32,128]{2,1,0:T(8,128)(2,1)} %bitcast.8, ...), custom_call_target="tpu_custom_call" | custom-call | tf_op jit(solution)/shard_map/pallas_call | solution.py:375
  40.0 0.0 copy-done.1
  40.0 0.0 copy-start
  40.0 1.0 %copy-done = bf16[256,1024]{1,0:T(8,128)(2,1)S(1)} copy-done((bf16[256,1024]{1,0:T(8,128)(2,1)S(1)}, bf16[256,1024]{1,0:T(8,128)(2,1)}, u32[]{:S(2)}) %copy-start) | copy-done | bytes 524312
  41.0 1.9 %shard_map.123 = (bf16[64,1024]{1,0:T(8,128)(2,1)}, f32[64,1024]{1,0:T(8,128)}) custom-call(s32[1,1024]{1,0:T(1,128)S(1)} %copy-done.1, bf16[256,1024]{1,0:T(8,128)(2,1)S(1)} %copy-done), custom_call_target="tpu_custom_call" | custom-call | tf_op jit(solution)/shard_map/pallas_call | solution.py:428
Async XLA Ops:
  0.6 39.3 %copy-start.1 = (s32[1,1024]{1,0:T(1,128)S(1)}, s32[1,1024]{1,0:T(1,128)}, u32[]{:S(2)}) copy-start(s32[1,1024]{1,0:T(1,128)} %order.3) | copy-start | bytes 12292
  40.0 1.0 %copy-start = (bf16[256,1024]{1,0:T(8,128)(2,1)S(1)}, bf16[256,1024]{1,0:T(8,128)(2,1)}, u32[]{:S(2)}) copy-start(bf16[256,1024]{1,0:T(8,128)(2,1)} %shard_map.122.parts) | copy-start | bytes 1572868

commit v6 on v5

--- a/solution.py
+++ b/solution.py
@@ -10,7 +10,7 @@
 BF = jnp.bfloat16
 F32 = jnp.float32
 GROUP = 4
-NEAR_GROUP = 16
+NEAR_GROUP = 32
 
 
 def dot(a, b, ca, cb):
@@ -110,43 +110,6 @@
         lslot[pl.ds(g * GROUP, GROUP)] = placed[:, leaf:].reshape(GROUP, wide, leaf)
 
     rin[me] = rslot[me]
-    pl.semaphore_wait(barrier, n - 1)
-
-    groups = n // GROUP
-
-    def each(first, act):
-        for k in range(GROUP):
-            other = first + lax.rem(me + k, GROUP)
-
-            @pl.when(other != me)
-            def _():
-                act(other)
-
-    def group_at(g):
-        return lax.rem(me // GROUP + g, groups) * GROUP
-
-    def r_copy(t):
-        return send(rslot.at[t], rin.at[me], r_send.at[t], r_recv.at[me], t)
-
-    def r_arrival(t):
-        return send(rslot.at[me], rin.at[t], r_send.at[t], r_recv.at[t], t)
-
-    def c_copy(t):
-        return send(cbuf.at[t], cin.at[me], c_send.at[t], c_recv.at[me], t)
-
-    def c_arrival(t):
-        return send(cbuf.at[t], cin.at[t], c_send.at[t], c_recv.at[t], t)
-
-    def a_copy(t):
-        return send(abuf.at[t], ain.at[me], a_send.at[t], a_recv.at[me], t)
-
-    def a_arrival(t):
-        return send(abuf.at[t], ain.at[t], a_send.at[t], a_recv.at[t], t)
-
-    @pl.loop(0, groups)
-    def _(g):
-        each(group_at(g), lambda t: r_copy(t).start())
-
     pt[...] = (
         lax.broadcasted_iota(jnp.int32, (panels, panels), 0) == order[...]
     ).astype(F32).astype(BF)
@@ -155,6 +118,43 @@
     for c in range(cl):
         ext[c + 1] = sorted_t[:exc, c * leaf : (c + 1) * leaf]
         want[pl.ds(c * exc, exc), :] = sorted_t[exc:, c * leaf : (c + 1) * leaf].astype(F32)
+
+    pl.semaphore_wait(barrier, n - 1)
+
+    groups = n // GROUP
+
+    def each(first, act):
+        for k in range(GROUP):
+            other = first + lax.rem(me + k, GROUP)
+
+            @pl.when(other != me)
+            def _():
+                act(other)
+
+    def group_at(g):
+        return lax.rem(me // GROUP + g, groups) * GROUP
+
+    def r_copy(t):
+        return send(rslot.at[t], rin.at[me], r_send.at[t], r_recv.at[me], t)
+
+    def r_arrival(t):
+        return send(rslot.at[me], rin.at[t], r_send.at[t], r_recv.at[t], t)
+
+    def c_copy(t):
+        return send(cbuf.at[t], cin.at[me], c_send.at[t], c_recv.at[me], t)
+
+    def c_arrival(t):
+        return send(cbuf.at[t], cin.at[t], c_send.at[t], c_recv.at[t], t)
+
+    def a_copy(t):
+        return send(abuf.at[t], ain.at[me], a_send.at[t], a_recv.at[me], t)
+
+    def a_arrival(t):
+        return send(abuf.at[t], ain.at[t], a_send.at[t], a_recv.at[t], t)
+
+    @pl.loop(0, groups)
+    def _(g):
+        each(group_at(g), lambda t: r_copy(t).start())
 
     to_left = send(ext.at[1], ext.at[cl + 1], e_send.at[0], e_recv.at[0], left)
     to_right = send(ext.at[cl], ext.at[0], e_send.at[1], e_recv.at[1], right)

time: 43.1 us -> 42.5 us (0.986)
  Pallas kernels: 41.2 us -> 40.6 us
    pallas_call x1, Pallas kernels: 39.3 us -> 38.7 us  [shards(): pl.pallas_call(functools.partial(kernel, n), out_shape=jax.ShapeDtypeStru...]
where the time goes in v6:
time: 42.5 us; the launch traced here: 42.3 us
  Pallas kernels  40.6 us (96%)
  local copies, waits for them, and re-layouts  1.04 us (2%)
  between operations  0.67 us (2%)
    pallas_call x1, Pallas kernels, shards(): pl.pallas_call(functools.partial(kernel, n), out_shape=jax.ShapeDtypeStru...  38.7 us
    pallas_call x1, Pallas kernels, shards(): pl.pallas_call(unsort, out_shape=(jax.ShapeDtypeStruct((exc, panels), BF)...  1.87 us
    unnamed x4, local copies, waits for them, and re-layouts  1.04 us

profile of v6, /device:TPU:1, one launch (start us, length us, event | category | flops | bytes accessed | tf_op | source)
XLA Modules:
  0.0 42.3 jit_solution(13388814498466680494)
XLA Ops:
  0.6 0.0 copy-start.1
  0.6 38.7 %shard_map.122.parts = bf16[256,1024]{1,0:T(8,128)(2,1)} custom-call(bf16[64,1024]{1,0:T(8,128)(2,1)} %bitcast.6, bf16[64,1024]{1,0:T(8,128)(2,1)} %bitcast.7, s32[1,1024]{1,0:T(1,128)} %order.3, bf16[64,128,128]{2,1,0:T(8,128)(2,1)} %near_hbm.1, s32[64]{0:T(128)} %nrows.1, s32[64]{0:T(128)} %ncols.1, bf16[16,32,128]{2,1,0:T(8,128)(2,1)} %bitcast.8, ...), custom_call_target="tpu_custom_call" | custom-call | tf_op jit(solution)/shard_map/pallas_call | solution.py:375
  39.4 0.0 copy-done.1
  39.4 0.0 copy-start
  39.4 1.0 %copy-done = bf16[256,1024]{1,0:T(8,128)(2,1)S(1)} copy-done((bf16[256,1024]{1,0:T(8,128)(2,1)S(1)}, bf16[256,1024]{1,0:T(8,128)(2,1)}, u32[]{:S(2)}) %copy-start) | copy-done | bytes 524312
  40.4 1.9 %shard_map.123 = (bf16[64,1024]{1,0:T(8,128)(2,1)}, f32[64,1024]{1,0:T(8,128)}) custom-call(s32[1,1024]{1,0:T(1,128)S(1)} %copy-done.1, bf16[256,1024]{1,0:T(8,128)(2,1)S(1)} %copy-done), custom_call_target="tpu_custom_call" | custom-call | tf_op jit(solution)/shard_map/pallas_call | solution.py:428
Async XLA Ops:
  0.6 38.7 %copy-start.1 = (s32[1,1024]{1,0:T(1,128)S(1)}, s32[1,1024]{1,0:T(1,128)}, u32[]{:S(2)}) copy-start(s32[1,1024]{1,0:T(1,128)} %order.3) | copy-start | bytes 12292
  39.4 1.0 %copy-start = (bf16[256,1024]{1,0:T(8,128)(2,1)S(1)}, bf16[256,1024]{1,0:T(8,128)(2,1)}, u32[]{:S(2)}) copy-start(bf16[256,1024]{1,0:T(8,128)(2,1)} %shard_map.122.parts) | copy-start | bytes 1572868
